TPU v7x, 512 devices: a whole 4x4x16 slice. The times are simulated.
512 devices in a mesh: gx: 128 (over z, y, core), gz: 4 (over x).
Axes of the slice: x: 4, y: 4, z: 16, core: 2. Of those that a mesh axis runs over, the one named last changes fastest.
Arguments:
- level_set: float32 [8192, 4096], P(('gx', 'gz')), may hold values from -60 to 60
- neighbours: int32 [8192, 6], P(('gx', 'gz')), may hold values from -1 to 8191, as said below
- live_count: int32 [512], P(('gx', 'gz')), may hold values from 4 to 16, as said below
- dense_target: int32 [8192], P(('gx', 'gz')), may hold values from -1 to 31, as said below
Outputs:
- level_set_out: float32 [8192, 4096], P(('gx', 'gz'))
- force_grid: float32 [512, 3, 16, 256], P('gx', None, 'gz')
Inputs may be any that keep to these rules, and one draw needn't show every extreme that they name: `live_count`: some device holds 16 live bricks. `neighbours`: -1 or the global slot of a live brick on a device of the same gz index whose gx index differs from the own by 1 to 3, by 0, or by exactly 128 / 2 counted round; rows of dead slots are all -1; the entries of one device that name bricks of one other gx index number at most 4, and every device reaches that for some gx index. `dense_target`: -1 exactly on dead slots.
All inputs are finite; a program needn't handle non-finite values.
Results may differ from a plain program's by a relative error of at most 0.0003.
Values sent between devices are 32-bit elements; how exact they have to be, the bound alone decides.
A program may use at most 64 MiB of HBM per device.

v0:
```python
import math

import jax
import jax.numpy as jnp
import numpy as np
from jax import lax
from jax.sharding import PartitionSpec as P

SIDE = 16
CAP_H = 4
DN_DEV = 4
STEPS = 3


STEP_SIZE = 0.3
WENO_EPS = 1e-06
BAND_WIDTH = 1.5
OPPOSITE = np.array([1, 0, 3, 2, 5, 4], np.int32)


def to_strips(values, axis_id):
    leading = values.shape[:-1]
    block_cube = values.reshape(leading + (SIDE, SIDE, SIDE))
    if axis_id == 1:
        block_cube = jnp.swapaxes(block_cube, -3, -2)
    elif axis_id == 2:
        block_cube = jnp.moveaxis(block_cube, -1, -3)
    return block_cube.reshape(leading + (SIDE, SIDE * SIDE))


def from_strips(strips, axis_id):
    leading = strips.shape[:-2]
    block_cube = strips.reshape(leading + (SIDE, SIDE, SIDE))
    if axis_id == 1:
        block_cube = jnp.swapaxes(block_cube, -3, -2)
    elif axis_id == 2:
        block_cube = jnp.moveaxis(block_cube, -3, -1)
    return block_cube.reshape(leading + (SIDE * SIDE * SIDE,))


def face_table(surface, layers):
    pieces = []
    for axis_id in range(3):
        strips = to_strips(surface, axis_id)
        pieces.append(strips[:, :layers])
        pieces.append(strips[:, SIDE - layers :])
    stacked = jnp.stack(pieces, 1)
    return stacked.reshape(surface.shape[0] * 6, layers * SIDE * SIDE)


def square(values):
    return values * values


def weno(first, second, middle, fourth, fifth):
    stencil_one = first / 3.0 - 7.0 * second / 6.0 + 11.0 * middle / 6.0
    stencil_two = -second / 6.0 + 5.0 * middle / 6.0 + fourth / 3.0
    stencil_three = middle / 3.0 + 5.0 * fourth / 6.0 - fifth / 6.0
    smooth_one = 13.0 / 12.0 * square(first - 2.0 * second + middle) + 0.25 * square(
        first - 4.0 * second + 3.0 * middle
    )
    smooth_two = 13.0 / 12.0 * square(second - 2.0 * middle + fourth) + 0.25 * square(
        second - fourth
    )
    smooth_three = 13.0 / 12.0 * square(middle - 2.0 * fourth + fifth) + 0.25 * square(
        3.0 * middle - 4.0 * fourth + fifth
    )
    weight_one = 0.1 / square(WENO_EPS + smooth_one)
    weight_two = 0.6 / square(WENO_EPS + smooth_two)
    weight_three = 0.3 / square(WENO_EPS + smooth_three)
    combined = weight_one * stencil_one + weight_two * stencil_two + weight_three * stencil_three
    return combined / (weight_one + weight_two + weight_three)


def extend(strips, ghost_low, ghost_high, missing_low, missing_high):
    low_side = jnp.where(
        missing_low[:, None, None], jnp.broadcast_to(strips[:, :1], ghost_low.shape), ghost_low
    )
    high_side = jnp.where(
        missing_high[:, None, None],
        jnp.broadcast_to(strips[:, SIDE - 1 :], ghost_high.shape),
        ghost_high,
    )
    return jnp.concatenate([low_side, strips, high_side], 1)


def reinit_step(surface, start, ghosts, missing):
    sign_speed = start / jnp.sqrt(start * start + 1.0)
    grad_sq = jnp.zeros_like(surface)
    for axis_id in range(3):
        strips = to_strips(surface, axis_id)
        extended = extend(
            strips,
            ghosts[:, 2 * axis_id],
            ghosts[:, 2 * axis_id + 1],
            missing[:, 2 * axis_id],
            missing[:, 2 * axis_id + 1],
        )
        differences = extended[:, 1:] - extended[:, :-1]
        upwind_left = weno(
            differences[:, 0:SIDE],
            differences[:, 1 : SIDE + 1],
            differences[:, 2 : SIDE + 2],
            differences[:, 3 : SIDE + 3],
            differences[:, 4 : SIDE + 4],
        )
        upwind_right = weno(
            differences[:, 5 : SIDE + 5],
            differences[:, 4 : SIDE + 4],
            differences[:, 3 : SIDE + 3],
            differences[:, 2 : SIDE + 2],
            differences[:, 1 : SIDE + 1],
        )
        outward = jnp.maximum(
            square(jnp.maximum(upwind_left, 0.0)), square(jnp.minimum(upwind_right, 0.0))
        )
        inward = jnp.maximum(
            square(jnp.minimum(upwind_left, 0.0)), square(jnp.maximum(upwind_right, 0.0))
        )
        chosen = jnp.where(to_strips(start, axis_id) > 0.0, outward, inward)
        grad_sq = grad_sq + from_strips(chosen, axis_id)
    return surface - STEP_SIZE * sign_speed * (jnp.sqrt(grad_sq) - 1.0)


def force_of(surface, rim_layers, missing):
    laplace = jnp.zeros_like(surface)
    gradient = []
    for axis_id in range(3):
        strips = to_strips(surface, axis_id)
        extended = extend(
            strips,
            rim_layers[:, 2 * axis_id],
            rim_layers[:, 2 * axis_id + 1],
            missing[:, 2 * axis_id],
            missing[:, 2 * axis_id + 1],
        )
        laplace = laplace + from_strips(
            extended[:, 2:] - 2.0 * extended[:, 1:-1] + extended[:, :-2], axis_id
        )
        gradient.append(from_strips(0.5 * (extended[:, 2:] - extended[:, :-2]), axis_id))
    smeared_delta = jnp.where(
        jnp.abs(surface) < BAND_WIDTH,
        (1.0 + jnp.cos(math.pi * surface / BAND_WIDTH)) / (2.0 * BAND_WIDTH),
        0.0,
    )
    forces = jnp.stack(gradient, 1) * (laplace * smeared_delta)[:, None, :]
    half_side = SIDE // 2
    coarsened = forces.reshape(surface.shape[0], 3, half_side, 2, half_side, 2, half_side, 2).mean(
        axis=(3, 5, 7)
    )
    return coarsened.reshape(surface.shape[0], 3 * half_side**3)


def place_octants(gathered, dense_count):
    half_side = SIDE // 2
    shaped = gathered.reshape(dense_count, 2, 2, 2, 3, half_side, half_side, half_side)
    moved = jnp.transpose(shaped, (0, 4, 3, 7, 1, 5, 2, 6))
    return moved.reshape(dense_count, 3, SIDE, SIDE * SIDE)


def shards(level_set, neighbours, live_count, dense_target):
    slot_count = level_set.shape[0]
    peer_count = lax.axis_size("gx")
    layer_count = lax.axis_size("gz")
    my_column = lax.axis_index("gx")
    missing = neighbours < 0
    target = jnp.where(missing, 0, neighbours)
    target_col = target // slot_count // layer_count
    remote = jnp.logical_and(jnp.logical_not(missing), target_col != my_column)
    wanted = (target % slot_count * 6 + OPPOSITE[None, :]).astype(jnp.int32)
    flat_remote = remote.reshape(-1)
    flat_col = target_col.reshape(-1)
    matches = jnp.logical_and(
        flat_col[:, None] == jnp.arange(peer_count)[None, :], flat_remote[:, None]
    ).astype(jnp.int32)
    arrival = jnp.sum(jnp.cumsum(matches, 0) * matches, 1) - 1
    local_row = jnp.where(remote, 0, wanted).reshape(-1)
    box_count = peer_count * CAP_H
    box_slot = jnp.where(flat_remote, flat_col * CAP_H + arrival, box_count)
    request = (
        jnp.full((box_count,), -1, jnp.int32).at[box_slot].set(wanted.reshape(-1), mode="drop")
    )
    incoming = lax.all_to_all(
        request.reshape(peer_count, CAP_H), "gx", split_axis=0, concat_axis=0, tiled=True
    ).reshape(-1)
    served = incoming >= 0
    source_row = jnp.where(served, incoming, 0)
    remote_row = jnp.where(flat_remote, box_slot, 0)

    def answer(faces_now):
        return jnp.where(served[:, None], faces_now[source_row], 0.0).reshape(
            box_count // CAP_H, CAP_H, -1
        )

    def collect(faces_now, returned, layers):
        arrived = returned.reshape(box_count, -1)[remote_row]
        rows_all = jnp.where(flat_remote[:, None], arrived, faces_now[local_row])
        return rows_all.reshape(slot_count, 6, layers, SIDE * SIDE)

    surface = level_set
    for pseudo_step in range(STEPS):
        fetch_faces_now = face_table(surface, 3)
        answers = answer(fetch_faces_now)
        fetch_returned = lax.all_to_all(answers, "gx", split_axis=0, concat_axis=0, tiled=True)
        surface = reinit_step(
            surface, level_set, collect(fetch_faces_now, fetch_returned, 3), missing
        )
    faces_rim = face_table(surface, 1)
    rim_answers = answer(faces_rim)
    rim_returned = lax.all_to_all(rim_answers, "gx", split_axis=0, concat_axis=0, tiled=True)
    rim_layers = collect(faces_rim, rim_returned, 1)
    coarsened = force_of(surface, rim_layers, missing)
    is_live = jnp.arange(slot_count) < live_count[0]
    level_set_out = jnp.where(is_live[:, None], surface, 0.0)
    selector = (dense_target[:, None] == jnp.arange(DN_DEV * 8)[None, :]).astype(jnp.float32)
    gathered = jnp.dot(
        selector.T, coarsened, precision=lax.Precision.HIGHEST, preferred_element_type=jnp.float32
    )
    dense_part = place_octants(gathered, DN_DEV)
    force_grid = lax.psum_scatter(dense_part, "gz", scatter_dimension=2, tiled=True)
    return (level_set_out, force_grid)


def solution(mesh):
    placed = (P(("gx", "gz"), None), P(("gx", "gz"), None), P(("gx", "gz")), P(("gx", "gz")))
    return jax.shard_map(
        shards,
        mesh=mesh,
        in_specs=placed,
        out_specs=(P(("gx", "gz"), None), P("gx", None, "gz", None)),
        check_vma=False,
    )
```

profile of v0, /device:TPU:1, one launch (start us, length us, event | category | flops | bytes accessed | tf_op | source)
XLA Modules:
  0.0 560.4 jit_solution(7184804935560379889)
XLA Ops:
  11.1 20.6 %all-to-all-start = ((s32[128,1,4]{2,1,0:T(1,128)}), s32[128,1,4]{2,1,0:T(1,128)S(1)}, u32[]{:S(2)}, u32[]{:S(2)}) async-start(s32[128,1,4]{2,1,0:T(1,128)} %bitcast.4), calls=%async_computation | async-start | bytes 131072 | tf_op jit(solution)/shard_map/all_to_all | solution.py:183
  47.9 2.6 gather_fusion
  54.2 15.4 %all-to-all-start.1 = ((f32[128,4,768]{2,1,0:T(4,128)}), f32[128,4,768]{2,1,0:T(4,128)}, u32[]{:S(2)}, u32[]{:S(2)}) async-start(f32[128,4,768]{2,1,0:T(4,128)} %broadcast_select_fusion.2), calls=%async_computation.1 | async-start | bytes 3145728 | tf_op jit(solution)/shard_map/all_to_all | solution.py:204
  70.8 72.2 %all-to-all-done.1 = f32[128,4,768]{2,1,0:T(4,128)} async-done(((f32[128,4,768]{2,1,0:T(4,128)}), f32[128,4,768]{2,1,0:T(4,128)}, u32[]{:S(2)}, u32[]{:S(2)}) %all-to-all-start.1) | async-done | bytes 1572896 | tf_op jit(solution)/shard_map/all_to_all | solution.py:204
  151.1 3.2 reshape.457
  162.9 2.8 reshape.461
  169.7 2.8 gather_fusion.3
  175.8 11.3 %all-to-all-start.2 = ((f32[128,4,768]{2,1,0:T(4,128)}), f32[128,4,768]{2,1,0:T(4,128)}, u32[]{:S(2)}, u32[]{:S(2)}) async-start(f32[128,4,768]{2,1,0:T(4,128)} %broadcast_select_fusion.1), calls=%async_computation.2 | async-start | bytes 3145728 | tf_op jit(solution)/shard_map/all_to_all | solution.py:204
  188.3 72.2 %all-to-all-done.2 = f32[128,4,768]{2,1,0:T(4,128)} async-done(((f32[128,4,768]{2,1,0:T(4,128)}), f32[128,4,768]{2,1,0:T(4,128)}, u32[]{:S(2)}, u32[]{:S(2)}) %all-to-all-start.2) | async-done | bytes 1572896 | tf_op jit(solution)/shard_map/all_to_all | solution.py:204
  270.2 3.2 reshape.466
  283.1 2.6 reshape.470
  289.7 2.8 gather_fusion.6
  295.8 11.3 %all-to-all-start.3 = ((f32[128,4,768]{2,1,0:T(4,128)}), f32[128,4,768]{2,1,0:T(4,128)}, u32[]{:S(2)}, u32[]{:S(2)}) async-start(f32[128,4,768]{2,1,0:T(4,128)} %broadcast_select_fusion), calls=%async_computation.3 | async-start | bytes 3145728 | tf_op jit(solution)/shard_map/all_to_all | solution.py:204
  309.5 71.0 %all-to-all-done.3 = f32[128,4,768]{2,1,0:T(4,128)} async-done(((f32[128,4,768]{2,1,0:T(4,128)}), f32[128,4,768]{2,1,0:T(4,128)}, u32[]{:S(2)}, u32[]{:S(2)}) %all-to-all-start.3) | async-done | bytes 1572896 | tf_op jit(solution)/shard_map/all_to_all | solution.py:204
  390.2 3.2 reshape.475
  403.8 2.8 reshape.479
  410.4 11.0 %all-to-all-start.4 = ((f32[128,4,256]{2,1,0:T(4,128)}), f32[128,4,256]{2,1,0:T(4,128)S(1)}, u32[]{:S(2)}, u32[]{:S(2)}) async-start(f32[128,4,256]{2,1,0:T(4,128)} %broadcast_select_fusion.3), calls=%async_computation.4 | async-start | bytes 1048576 | tf_op jit(solution)/shard_map/all_to_all | solution.py:210
  422.4 29.8 %all-to-all-done.4 = f32[128,4,256]{2,1,0:T(4,128)S(1)} async-done(((f32[128,4,256]{2,1,0:T(4,128)}), f32[128,4,256]{2,1,0:T(4,128)S(1)}, u32[]{:S(2)}, u32[]{:S(2)}) %all-to-all-start.4) | async-done | bytes 524320 | tf_op jit(solution)/shard_map/all_to_all | solution.py:210
  459.1 3.8 reshape.486
  478.8 7.7 %fusion = f32[16,3,8,8,8]{0,4,3,2,1:T(8,128)S(1)} fusion(f32[16,1,8,2,8,2,8,2]{0,7,6,5,4,3,2,1:T(2,128)} %bitcast.426, f32[16,1,8,2,8,2,8,2]{0,7,6,5,4,3,2,1:T(2,128)} %bitcast.425, f32[16,1,8,2,8,2,8,2]{0,7,6,5,4,3,2,1:T(2,128)} %bitcast.424, f32[16,8,2,8,2,8,2]{0,6,5,4,3,2,1:T(2,128)S(1)} %bitcast.423), kind=kLoop, calls=%fused_computation.14 | loop fusion | flops 761856 | bytes 1146880 | tf_op jit(solution)/shard_map/reduce_sum | solution.py:148
  486.5 6.6 %convolution_bitcast_fusion = f32[4,3,2,8,2,8,2,8]{3,0,7,5,1,2,6,4:T(4,128)S(1)} fusion(f32[16,3,8,8,8]{0,4,3,2,1:T(8,128)S(1)} %fusion, s32[4,2,2,2]{0,3,2,1:T(2,128)S(1)} %multiply_add_fusion, s32[16]{0:T(128)S(1)} %copy-done.53), kind=kOutput, calls=%fused_computation.20 | convolution fusion | flops 9462272 | bytes 295104 | tf_op jit(solution)/shard_map/dot_general | solution.py:216
  493.1 3.9 copy.272
  497.0 6.1 %reshape.489 = f32[4,3,16,256]{3,2,1,0:T(8,128)} reshape(f32[4,3,2,8,2,8,2,8]{7,6,5,4,3,2,1,0:T(2,128)} %copy.272) | data formatting | bytes 393216 | tf_op jit(solution)/shard_map/reshape | solution.py:158
  505.1 46.8 %all-reduce.3.cloned.1.call-done = f32[4,3,16,256]{3,2,1,0:T(8,128)} async-done(((f32[4,3,16,256]{3,2,1,0:T(8,128)}), f32[4,3,16,256]{3,2,1,0:T(8,128)}) %all-reduce.3.cloned.1.call-update) | async-done | bytes 196624
  (314 shorter events, 127.6 us)
Async XLA Ops:
  8.0 137.9 %copy-start.20 = (pred[16,6]{1,0:T(8,128)(4,1)}, pred[16,6]{1,0:T(8,128)(4,1)S(1)}, u32[]{:S(2)}) copy-start(pred[16,6]{1,0:T(8,128)(4,1)S(1)} %copy.309) | copy-start | bytes 292
  11.1 35.4 %all-to-all-start = ((s32[128,1,4]{2,1,0:T(1,128)}), s32[128,1,4]{2,1,0:T(1,128)S(1)}, u32[]{:S(2)}, u32[]{:S(2)}) async-start(s32[128,1,4]{2,1,0:T(1,128)} %bitcast.4), calls=%async_computation | async-start | bytes 131072 | tf_op jit(solution)/shard_map/all_to_all | solution.py:183
  37.2 4.8 copy-start
  47.9 21.9 %copy-start.51 = (s32[1024]{0:T(1024)}, s32[1024]{0:T(1024)S(1)}, u32[]{:S(2)}) copy-start(s32[1024]{0:T(1024)S(1)} %get-tuple-element.87) | copy-start | bytes 12292
  54.2 88.8 %all-to-all-start.1 = ((f32[128,4,768]{2,1,0:T(4,128)}), f32[128,4,768]{2,1,0:T(4,128)}, u32[]{:S(2)}, u32[]{:S(2)}) async-start(f32[128,4,768]{2,1,0:T(4,128)} %broadcast_select_fusion.2), calls=%async_computation.1 | async-start | bytes 3145728 | tf_op jit(solution)/shard_map/all_to_all | solution.py:204
  69.6 75.4 %copy-start.52 = (s32[1024]{0:T(1024)}, s32[1024]{0:T(1024)S(1)}, u32[]{:S(2)}) copy-start(s32[1024]{0:T(1024)S(1)} %pad_clamp_fusion.1) | copy-start | bytes 12292
  69.6 76.5 %copy-start.27 = (pred[16]{0:T(512)(128)(4,1)}, pred[16]{0:T(512)(128)(4,1)S(1)}, u32[]{:S(2)}) copy-start(pred[16]{0:T(512)(128)(4,1)S(1)} %get-tuple-element.81) | copy-start | bytes 52
  69.7 76.5 %copy-start.31 = (pred[16]{0:T(512)(128)(4,1)}, pred[16]{0:T(512)(128)(4,1)S(1)}, u32[]{:S(2)}) copy-start(pred[16]{0:T(512)(128)(4,1)S(1)} %get-tuple-element.82) | copy-start | bytes 52
  69.7 76.5 %copy-start.35 = (pred[16]{0:T(512)(128)(4,1)}, pred[16]{0:T(512)(128)(4,1)S(1)}, u32[]{:S(2)}) copy-start(pred[16]{0:T(512)(128)(4,1)S(1)} %get-tuple-element.83) | copy-start | bytes 52
  69.7 76.5 %copy-start.39 = (pred[16]{0:T(512)(128)(4,1)}, pred[16]{0:T(512)(128)(4,1)S(1)}, u32[]{:S(2)}) copy-start(pred[16]{0:T(512)(128)(4,1)S(1)} %get-tuple-element.84) | copy-start | bytes 52
  69.7 76.5 %copy-start.43 = (pred[16]{0:T(512)(128)(4,1)}, pred[16]{0:T(512)(128)(4,1)S(1)}, u32[]{:S(2)}) copy-start(pred[16]{0:T(512)(128)(4,1)S(1)} %get-tuple-element.85) | copy-start | bytes 52
  69.7 76.5 %copy-start.47 = (pred[16]{0:T(512)(128)(4,1)}, pred[16]{0:T(512)(128)(4,1)S(1)}, u32[]{:S(2)}) copy-start(pred[16]{0:T(512)(128)(4,1)S(1)} %get-tuple-element.86) | copy-start | bytes 52
  175.8 84.7 %all-to-all-start.2 = ((f32[128,4,768]{2,1,0:T(4,128)}), f32[128,4,768]{2,1,0:T(4,128)}, u32[]{:S(2)}, u32[]{:S(2)}) async-start(f32[128,4,768]{2,1,0:T(4,128)} %broadcast_select_fusion.1), calls=%async_computation.2 | async-start | bytes 3145728 | tf_op jit(solution)/shard_map/all_to_all | solution.py:204
  295.8 84.7 %all-to-all-start.3 = ((f32[128,4,768]{2,1,0:T(4,128)}), f32[128,4,768]{2,1,0:T(4,128)}, u32[]{:S(2)}, u32[]{:S(2)}) async-start(f32[128,4,768]{2,1,0:T(4,128)} %broadcast_select_fusion), calls=%async_computation.3 | async-start | bytes 3145728 | tf_op jit(solution)/shard_map/all_to_all | solution.py:204
  410.4 42.9 %copy-start.21 = (pred[16,6]{1,0:T(8,128)(4,1)S(1)}, pred[16,6]{1,0:T(8,128)(4,1)}, u32[]{:S(2)}) copy-start(pred[16,6]{1,0:T(8,128)(4,1)} %copy-done.20) | copy-start | bytes 292
  410.4 41.8 %all-to-all-start.4 = ((f32[128,4,256]{2,1,0:T(4,128)}), f32[128,4,256]{2,1,0:T(4,128)S(1)}, u32[]{:S(2)}, u32[]{:S(2)}) async-start(f32[128,4,256]{2,1,0:T(4,128)} %broadcast_select_fusion.3), calls=%async_computation.4 | async-start | bytes 1048576 | tf_op jit(solution)/shard_map/all_to_all | solution.py:210
  421.4 32.0 %copy-start.30 = (pred[16]{0:T(512)(128)(4,1)S(1)}, pred[16]{0:T(512)(128)(4,1)}, u32[]{:S(2)}) copy-start(pred[16]{0:T(512)(128)(4,1)} %copy-done.27) | copy-start | bytes 52
  421.4 32.0 %copy-start.34 = (pred[16]{0:T(512)(128)(4,1)S(1)}, pred[16]{0:T(512)(128)(4,1)}, u32[]{:S(2)}) copy-start(pred[16]{0:T(512)(128)(4,1)} %copy-done.31) | copy-start | bytes 52
  421.4 32.0 %copy-start.38 = (pred[16]{0:T(512)(128)(4,1)S(1)}, pred[16]{0:T(512)(128)(4,1)}, u32[]{:S(2)}) copy-start(pred[16]{0:T(512)(128)(4,1)} %copy-done.35) | copy-start | bytes 52
  421.4 32.0 %copy-start.42 = (pred[16]{0:T(512)(128)(4,1)S(1)}, pred[16]{0:T(512)(128)(4,1)}, u32[]{:S(2)}) copy-start(pred[16]{0:T(512)(128)(4,1)} %copy-done.39) | copy-start | bytes 52
  421.5 32.0 %copy-start.46 = (pred[16]{0:T(512)(128)(4,1)S(1)}, pred[16]{0:T(512)(128)(4,1)}, u32[]{:S(2)}) copy-start(pred[16]{0:T(512)(128)(4,1)} %copy-done.43) | copy-start | bytes 52
  421.5 32.0 %copy-start.50 = (pred[16]{0:T(512)(128)(4,1)S(1)}, pred[16]{0:T(512)(128)(4,1)}, u32[]{:S(2)}) copy-start(pred[16]{0:T(512)(128)(4,1)} %copy-done.47) | copy-start | bytes 52
  421.5 130.4 %all-reduce.3.cloned.1.call-start = ((), (), s32[]{:S(2)}) async-start(), calls=%async_computation.5 | async-start | bytes 393216
  478.8 7.7 %copy-start.53 = (s32[16]{0:T(128)S(1)}, s32[16]{0:T(128)}, u32[]{:S(2)}) copy-start(s32[16]{0:T(128)} %param.8) | copy-start | bytes 196
  (37 other events, 91.2 us)
Sparse Core Ops, SparseCore 0:
  503.3 48.5 all-reduce.2
where the time goes:
time: 572 us; the launch traced here: 560 us
  waiting for transfers between devices  293 us (51%)
  local copies, waits for them, and re-layouts  135 us (24%)
  starting transfers between devices  69.6 us (12%)
  other arithmetic  39.4 us (7%)
  between operations  17.2 us (3%)
  matrix products  6.62 us (1%)
    all_to_all x3, waiting for transfers between devices, shards(): lax.all_to_all(answers, 'gx', split_axis=0, concat_axis=0, tiled=True)  215 us
    unnamed x2, waiting for transfers between devices  46.8 us
    all_to_all x3, starting transfers between devices, shards(): lax.all_to_all(answers, 'gx', split_axis=0, concat_axis=0, tiled=True)  38 us
    all_to_all x1, waiting for transfers between devices, shards(): lax.all_to_all(rim_answers, 'gx', split_axis=0, concat_axis=0, tiled=True)  29.8 us
    all_to_all x1, starting transfers between devices, shards(): lax.all_to_all(request.reshape(peer_count, CAP_H), 'gx', split_axis=0, co...  20.6 us
    reshape x8, local copies, waits for them, and re-layouts, from_strips(): return block_cube.reshape(leading + (SIDE * SIDE * SIDE,))  20.3 us
    reshape x15, local copies, waits for them, and re-layouts, from_strips(): block_cube = strips.reshape(leading + (SIDE, SIDE, SIDE))  20.1 us
    gather x8, local copies, waits for them, and re-layouts, answer(): faces_now[source_row]  15.1 us
  transfers between devices with their start and end apart: 6, of which 6 were waited for; matrix products, arithmetic and copies ran while one was open for 3% of the time, Pallas kernels for 0%

commit v1 on v0

v1 whole, which is shorter than its diff:
```python
import functools
import math

import jax
import jax.numpy as jnp
from jax import lax
from jax.experimental import pallas as pl
from jax.experimental.pallas import tpu as pltpu
from jax.sharding import PartitionSpec as P

SIDE = 16
SLOTS = 16
DENSE = 4
STEPS = 3
ROUNDS = STEPS + 1
BAND_WIDTH = 1.5
MESH = pl.DeviceIdType.MESH

PEERS = (0, 1, 2, 4, 5, 6, 7)
AXIS_ROWS = 512


def facing(peer):
    return 7 if peer == 7 else 6 - peer


def exchange(values, width, masks):
    count = len(values)
    bits = count.bit_length() - 1
    rolled = [v if j == 0 else pltpu.roll(v, j * width, 1) for j, v in enumerate(values)]
    moved = [rolled[-i % count] for i in range(count)]
    for bit in range(bits):
        moved = [jnp.where(masks[bit], moved[(i - (1 << bit)) % count], moved[i]) for i in range(count)]
    return [v if i == 0 else pltpu.roll(v, 128 - i * width, 1) for i, v in enumerate(moved)]


def lane_masks(rows, width, bits):
    lanes = lax.broadcasted_iota(jnp.int32, (rows, 128), 1)
    return [(lanes & (width << bit)) != 0 for bit in range(bits)]


def weno_axis(u, first, last, sigma, store):
    d = {j: u[j] - u[j - 1] for j in range(first - 2, last + 3)}
    e = {j: d[j + 1] - d[j] for j in range(first - 2, last + 2)}
    s = {j: e[j] - e[j - 1] for j in range(first - 1, last + 2)}
    t = {j: s[j + 1] - s[j] for j in range(first - 1, last + 1)}
    r1, r2, r3 = {}, {}, {}
    for j in range(first - 1, last + 2):
        base = (13.0 / 3.0) * (s[j] * s[j]) + 4e-6
        if j <= last - 1:
            lean = (e[j] + e[j]) + s[j]
            r = pltpu.reciprocal(base + lean * lean, approx=True)
            r1[j] = r * r
        if first <= j <= last:
            lean = e[j] + e[j - 1]
            r = pltpu.reciprocal(base + lean * lean, approx=True)
            r2[j] = 6.0 * (r * r)
        if j >= first + 1:
            lean = s[j] - (e[j - 1] + e[j - 1])
            r = pltpu.reciprocal(base + lean * lean, approx=True)
            r3[j] = r * r
    for i in range(first, last):
        half = 0.5 * t[i]
        left = 3.0 * d[i] + (e[i] + 0.5 * e[i - 1])
        right = left - half
        w3 = 3.0 * r3[i + 1]
        den = (r1[i - 1] + r2[i]) + w3
        num = r1[i - 1] * t[i - 1] + w3 * half
        left = left - num * pltpu.reciprocal(den, approx=True)
        w3 = 3.0 * r1[i]
        den = (r3[i + 2] + r2[i + 1]) + w3
        num = r3[i + 2] * t[i + 1] + w3 * half
        right = right + num * pltpu.reciprocal(den, approx=True)
        m = jnp.maximum(jnp.maximum(sigma(i) * left, -sigma(i) * right), 0.0)
        store(i, m * m)


def split3(x):
    hi = x.astype(jnp.bfloat16)
    rest = x - hi.astype(jnp.float32)
    mid = rest.astype(jnp.bfloat16)
    low = (rest - mid.astype(jnp.float32)).astype(jnp.bfloat16)
    return hi, mid, low


def as_one(mask):
    return jnp.where(mask, 1.0, 0.0).astype(jnp.bfloat16)


def dot_rows(a, b):
    return lax.dot_general(a, b, (((0,), (0,)), ((), ())), preferred_element_type=jnp.float32)


def dot(a, b):
    return lax.dot_general(a, b, (((1,), (0,)), ((), ())), preferred_element_type=jnp.float32)


def kernel(n_gx, n_gz, nb, live, target, start, level_out, part_out,
           u, faces, ghost, sigma, grad, speed, missing, near_col, far_col, force, request, heard,
           sends, recvs, fsend, frecv,
           request_sent, request_got, sent, got, fsent, fgot):
    me = lax.axis_index("gx")
    layer = lax.axis_index("gz")

    def peer_id(peer):
        step = n_gx // 2 if peer == 7 else peer - 3
        return {"gx": lax.rem(me + step + n_gx, n_gx)}

    barrier = pltpu.get_barrier_semaphore()
    for peer in PEERS:
        pl.semaphore_signal(barrier, inc=1, device_id=peer_id(peer), device_id_type=MESH)
    for turn in range(1, n_gz):
        pl.semaphore_signal(barrier, inc=1, device_id={"gz": lax.rem(layer + turn, n_gz)}, device_id_type=MESH)

    square_rows = lax.broadcasted_iota(jnp.int32, (128, 128), 0)
    square_lanes = lax.broadcasted_iota(jnp.int32, (128, 128), 1)
    entry = [jnp.broadcast_to(nb[:, side:side + 1], (16, 128)) for side in range(6)]
    entry = jnp.concatenate(entry + [jnp.full((32, 128), -1, jnp.int32)], 0)
    held = entry >= 0
    away = (entry >> (SLOTS * n_gz).bit_length() - 1) - me + 3
    kind = jnp.minimum(away & (n_gx - 1), 7)
    remote = jnp.logical_and(held, kind != 3)
    face = ((square_rows >> 4) ^ 1) * 16 + (entry & 15)
    mine = as_one(jnp.logical_and(remote, kind == square_lanes))
    before = dot(as_one(square_lanes < square_rows), mine)
    rank = dot((before * mine.astype(jnp.float32)).astype(jnp.bfloat16), jnp.ones((128, 128), jnp.bfloat16))
    slot = kind.astype(jnp.float32) * 8.0 + rank
    slot = jnp.where(remote, slot, -16.0)
    lane_ids = square_lanes.astype(jnp.float32)
    face = face.astype(jnp.float32)
    asked = dot_rows(as_one(slot == lane_ids), face.astype(jnp.bfloat16))
    asked = asked + dot_rows(as_one(slot + 4.0 == lane_ids), (face + 128.0).astype(jnp.bfloat16))
    request[...] = asked[:64].reshape(8, 8, 128)
    far_col[...] = slot[:96]
    near_col[...] = jnp.where(jnp.logical_and(held, kind == 3), face, -16.0)[:96]
    missing[...] = jnp.where(held, 0.0, 1.0)[:96]
    faces[96:, :] = jnp.zeros((32, 768), jnp.float32)

    pl.semaphore_wait(barrier, len(PEERS) + n_gz - 1)
    for peer in PEERS:
        pltpu.make_async_remote_copy(
            src_ref=request.at[peer], dst_ref=heard.at[facing(peer)],
            send_sem=request_sent.at[peer], recv_sem=request_got.at[facing(peer)],
            device_id=peer_id(peer), device_id_type=MESH).start()

    coarse_masks = lane_masks(16, 16, 3)
    fine_masks = lane_masks(16, 1, 4)

    def rows_of(axis, position, tile):
        return pl.ds(axis * AXIS_ROWS + position * 32 + tile * 16, 16)

    def keep_face(axis, position, tile, value):
        if 3 <= position < 13:
            return
        side = 2 * axis + (position >= 13)
        at = ((position % 13) * 2 + tile) * 128
        faces[side * 16:side * 16 + 16, at:at + 128] = value

    def spread(tile, x_of):
        ys = []
        for ytile in range(2):
            ys += exchange([x_of(i, ytile) for i in range(8)], 16, coarse_masks)
        for y in range(16):
            u[rows_of(1, y, tile), :] = ys[y]
            keep_face(1, y, tile, ys[y])
        zs = exchange(ys, 1, fine_masks)
        for z in range(16):
            u[rows_of(2, z, tile), :] = zs[z]
            keep_face(2, z, tile, zs[z])
        return ys, zs

    for tile in range(2):
        tops = {}
        for i in range(8):
            for ytile in range(2):
                x = tile * 8 + i
                value = start[:, x * 256 + ytile * 128:x * 256 + ytile * 128 + 128]
                u[rows_of(0, x, ytile), :] = value
                keep_face(0, x, ytile, value)
                sigma[rows_of(0, x, ytile), :] = jnp.where(value > 0.0, 1.0, -1.0)
                speed[rows_of(0, x, ytile), :] = 0.1 * value * lax.rsqrt(value * value + 1.0)
                tops[i, ytile] = value
        ys, zs = spread(tile, lambda i, ytile: tops[i, ytile])
        for p in range(16):
            sigma[rows_of(1, p, tile), :] = jnp.where(ys[p] > 0.0, 1.0, -1.0)
            sigma[rows_of(2, p, tile), :] = jnp.where(zs[p] > 0.0, 1.0, -1.0)

    for peer in PEERS:
        pltpu.make_async_remote_copy(
            src_ref=request.at[peer], dst_ref=heard.at[peer],
            send_sem=request_sent.at[peer], recv_sem=request_got.at[peer],
            device_id=peer_id(peer), device_id_type=MESH).wait()

    def copy_of(turn, peer, into):
        return pltpu.make_async_remote_copy(
            src_ref=sends.at[turn, peer], dst_ref=recvs.at[turn, into],
            send_sem=sent.at[turn, peer], recv_sem=got.at[turn, into],
            device_id=peer_id(peer), device_id_type=MESH)

    def serve(turn):
        hi, mid, low = split3(faces[...])
        cols = heard[...].reshape(64, 128)
        left = as_one(cols == lane_ids[:64])
        right = as_one(cols == lane_ids[:64] + 128.0)
        both = jnp.concatenate([left, left], 1)
        out = dot(both, jnp.concatenate([hi[:, :384], mid[:, :384]], 0))
        both = jnp.concatenate([right, right], 1)
        out = out + dot(both, jnp.concatenate([hi[:, 384:], mid[:, 384:]], 0))
        both = jnp.concatenate([left, right], 1)
        out = out + dot(both, jnp.concatenate([low[:, :384], low[:, 384:]], 0))
        sends[turn] = out.reshape(8, 8, 384)
        for peer in PEERS:
            copy_of(turn, peer, facing(peer)).start()
        near = as_one(near_col[...] == lane_ids[:96])
        out = dot(jnp.concatenate([near, near], 1), jnp.concatenate([hi, mid], 0)) + dot(near, low)
        for side in range(6):
            for part in range(6):
                at = (side * 6 + part) * 16
                ghost[at:at + 16, :] = out[side * 16:side * 16 + 16, part * 128:part * 128 + 128]

    def fetch(turn):
        for peer in PEERS:
            copy_of(turn, peer, peer).wait()
        hi, mid, low = split3(jnp.concatenate([recvs[turn, c] if c in PEERS else jnp.zeros((8, 384), jnp.float32)
                                               for c in range(8)], 0))
        arrived = jnp.concatenate([hi, mid, low, jnp.zeros_like(low)], 0)
        fold = jnp.where(lane_ids[:96] >= 64.0, lane_ids[:96] - 64.0, lane_ids[:96])
        for half in range(2):
            pick = as_one(far_col[...] + 4.0 * half == fold)
            out = dot(jnp.concatenate([pick, pick], 1), arrived)
            for side in range(6):
                for part in range(3):
                    at = (side * 6 + half * 3 + part) * 16
                    ghost[at:at + 16, :] += out[side * 16:side * 16 + 16, part * 128:part * 128 + 128]

    def column_rows(axis, position, column):
        return pl.ds(axis * AXIS_ROWS + position * 32 + column * 8, 8)

    def ghosts_at(axis, high, layer_id, column, edge):
        values = ghost[pl.ds((2 * axis + high) * 96 + layer_id * 32 + column * 8, 8), :]
        gone = missing[pl.ds((2 * axis + high) * 16 + (column % 2) * 8, 8), :]
        return jnp.where(gone > 0.0, edge, values)

    def weno_part(index, low, high):
        axis, column = index // 4, index % 4
        load = lambda i: u[column_rows(axis, i, column), :]
        signs = lambda i: sigma[column_rows(axis, i, column), :]

        def store(i, value):
            grad[column_rows(axis, i, column), :] = value

        if low == 3:
            values = {i: load(i) for i in range(16)}
            weno_axis(values, 3, 13, signs, store)
            return
        values = {i: load(i) for i in range(6)}
        for i in range(3):
            values[i - 3] = ghosts_at(axis, 0, i, column, values[0])
        weno_axis(values, 0, 3, signs, store)
        values = {i: load(i) for i in range(10, 16)}
        for i in range(3):
            values[16 + i] = ghosts_at(axis, 1, i, column, values[15])
        weno_axis(values, 13, 16, signs, store)

    def step(turn, carry):
        serve(turn)

        def inner(index, c):
            weno_part(index, 3, 13)
            return c

        def outer(index, c):
            weno_part(index, 0, 16)
            return c

        lax.fori_loop(0, 12, inner, 0)
        fetch(turn)
        lax.fori_loop(0, 12, outer, 0)

        for tile in range(2):
            sums = exchange([grad[rows_of(2, z, tile), :] for z in range(16)], 1, fine_masks)
            sums = [sums[y] + grad[rows_of(1, y, tile), :] for y in range(16)]
            fresh = {}
            for ytile in range(2):
                xs = exchange(sums[ytile * 8:ytile * 8 + 8], 16, coarse_masks)
                for i in range(8):
                    rows = rows_of(0, tile * 8 + i, ytile)
                    steep = jnp.sqrt(xs[i] + grad[rows, :])
                    value = u[rows, :] - speed[rows, :] * (steep - 3.0)
                    u[rows, :] = value
                    keep_face(0, tile * 8 + i, ytile, value)
                    fresh[i, ytile] = value
            spread(tile, lambda i, ytile: fresh[i, ytile])
        return carry

    lax.fori_loop(0, STEPS, step, 0)

    serve(STEPS)
    keep = lax.broadcasted_iota(jnp.int32, (16, 128), 0) < live[0]
    for x in range(16):
        for ytile in range(2):
            at = x * 256 + ytile * 128
            level_out[:, at:at + 128] = jnp.where(keep, u[rows_of(0, x, ytile), :], 0.0)
    fetch(STEPS)

    def rim(axis, high, tile, edge):
        values = ghost[pl.ds((2 * axis + high) * 96 + (2 - 2 * high) * 32 + tile * 16, 16), :]
        return jnp.where(missing[pl.ds((2 * axis + high) * 16, 16), :] > 0.0, edge, values)

    def beside(axis, position, tile):
        here = u[rows_of(axis, position, tile), :]
        low = rim(axis, 0, tile, here) if position == 0 else u[rows_of(axis, position - 1, tile), :]
        high = rim(axis, 1, tile, here) if position == 15 else u[rows_of(axis, position + 1, tile), :]
        return (high + low) - (here + here), high - low, here

    for tile in range(2):
        lap_y, grad_x = [], []
        for ytile in range(2):
            parts = [beside(0, tile * 8 + i, ytile) for i in range(8)]
            lap_y += exchange([p[0] for p in parts], 16, coarse_masks)
            grad_x += exchange([p[1] for p in parts], 16, coarse_masks)
        parts = [beside(1, y, tile) for y in range(16)]
        laps = exchange([lap_y[y] + parts[y][0] for y in range(16)], 1, fine_masks)
        grad_x = exchange(grad_x, 1, fine_masks)
        grad_y = exchange([p[1] for p in parts], 1, fine_masks)
        held = None
        for z in range(16):
            lap, grad_z, here = beside(2, z, tile)
            lap = lap + laps[z]
            v2 = jnp.minimum(here * here, BAND_WIDTH * BAND_WIDTH) * ((math.pi / 3.0) ** 2)
            wave = 1.0 / 479001600.0
            for power in (-1.0 / 3628800.0, 1.0 / 40320.0, -1.0 / 720.0, 1.0 / 24.0, -0.5, 1.0):
                wave = wave * v2 + power
            lap = jnp.where(jnp.abs(here) < BAND_WIDTH, lap * (wave * wave * (2.0 / 3.0)), 0.0)
            forces = [lap * grad_x[z], lap * grad_y[z], lap * grad_z]
            if z % 2 == 0:
                held = forces
            else:
                for a in range(3):
                    force[a, pl.ds(z // 2 * 16, 16), tile * 128:tile * 128 + 128] = held[a] + forces[a]

    r = lax.broadcasted_iota(jnp.int32, (256, 256), 0)
    l = lax.broadcasted_iota(jnp.int32, (256, 256), 1)
    same = jnp.logical_and((r >> 5) == ((l >> 4) & 7), ((r >> 1) & 7) == (l & 7))
    average = jnp.where(same, 1.0 / 16.0, 0.0).astype(jnp.bfloat16)
    lanes = lax.broadcasted_iota(jnp.int32, (16, 256), 1)
    brick_rows = lax.broadcasted_iota(jnp.int32, (16, 256), 0)
    lane_bricks = lax.broadcasted_iota(jnp.int32, (64, 128), 1)
    by_row = jnp.zeros((16, 256), jnp.int32)
    by_lane = jnp.full((64, 128), -1, jnp.int32)
    for b in range(16):
        by_row = jnp.where(brick_rows == b, target[b], by_row)
        by_lane = jnp.where((lane_bricks & 15) == b, target[b], by_lane)
    octant = jnp.logical_and(((by_row >> 2) & 1) == (lanes >> 7), ((by_row >> 1) & 1) == ((lanes >> 3) & 1))
    octant = jnp.where(octant, 1.0, 0.0)
    out_rows = lax.broadcasted_iota(jnp.int32, (64, 128), 0)
    pick = jnp.logical_and((by_lane >> 3) == (out_rows & 3), (by_lane & 1) == (out_rows >> 5))
    pick = jnp.logical_and(pick, (lane_bricks >> 4) == ((out_rows >> 2) & 7))
    pick = jnp.where(pick, 1.0, 0.0).astype(jnp.bfloat16)
    share = 64 // n_gz
    for a in range(3):
        hi, mid, low = split3(force[a])
        block = dot(hi, average) + (dot(mid, average) + dot(low, average))
        block = (block.reshape(8, 16, 256) * octant[None]).reshape(128, 256)
        hi, mid, low = split3(block)
        result = dot(pick, hi) + (dot(pick, mid) + dot(pick, low))
        for g in range(n_gz):
            fsend[g, a] = result[g * share:(g + 1) * share]

    def part_copy(turn):
        to = lax.rem(layer + turn, n_gz)
        return pltpu.make_async_remote_copy(
            src_ref=fsend.at[to], dst_ref=frecv.at[turn - 1],
            send_sem=fsent.at[turn - 1], recv_sem=fgot.at[turn - 1],
            device_id={"gz": to}, device_id_type=MESH)

    for turn in range(1, n_gz):
        part_copy(turn).start()
    total = fsend[layer]
    for turn in range(1, n_gz):
        part_copy(turn).wait()
        total = total + frecv[turn - 1]
    part_out[...] = total


def shards(n_gx, n_gz, level_set, neighbours, live_count, dense_target):
    share = 64 // n_gz
    smem = pl.BlockSpec(memory_space=pltpu.SMEM)
    vmem = pl.BlockSpec(memory_space=pltpu.VMEM)
    dma, f32 = pltpu.SemaphoreType.DMA, jnp.float32
    level, part = pl.pallas_call(
        functools.partial(kernel, n_gx, n_gz),
        out_shape=(jax.ShapeDtypeStruct(level_set.shape, f32), jax.ShapeDtypeStruct((3, share, 256), f32)),
        in_specs=[vmem, smem, smem, vmem],
        out_specs=(vmem, vmem),
        scratch_shapes=[
            pltpu.VMEM((3 * AXIS_ROWS, 128), f32),
            pltpu.VMEM((128, 768), f32),
            pltpu.VMEM((36 * 16, 128), f32),
            pltpu.VMEM((3 * AXIS_ROWS, 128), f32),
            pltpu.VMEM((3 * AXIS_ROWS, 128), f32),
            pltpu.VMEM((AXIS_ROWS, 128), f32),
            pltpu.VMEM((96, 128), f32),
            pltpu.VMEM((96, 128), f32),
            pltpu.VMEM((96, 128), f32),
            pltpu.VMEM((3, 128, 256), f32),
            pltpu.VMEM((8, 8, 128), f32),
            pltpu.VMEM((8, 8, 128), f32),
            pltpu.VMEM((ROUNDS, 8, 8, 384), f32),
            pltpu.VMEM((ROUNDS, 8, 8, 384), f32),
            pltpu.VMEM((n_gz, 3, share, 256), f32),
            pltpu.VMEM((n_gz - 1, 3, share, 256), f32),
            dma((8,)), dma((8,)), dma((ROUNDS, 8)), dma((ROUNDS, 8)), dma((n_gz - 1,)), dma((n_gz - 1,)),
        ],
        compiler_params=pltpu.CompilerParams(
            collective_id=0, has_side_effects=True, vmem_limit_bytes=24 << 20),
    )(neighbours, live_count, dense_target, level_set)
    part = part.reshape(3, SIDE // n_gz, DENSE, 256)
    return level, jnp.transpose(part, (2, 0, 1, 3))


def solution(mesh):
    placed = (P(("gx", "gz"), None), P(("gx", "gz"), None), P(("gx", "gz")), P(("gx", "gz")))
    return jax.shard_map(
        functools.partial(shards, mesh.shape["gx"], mesh.shape["gz"]),
        mesh=mesh,
        in_specs=placed,
        out_specs=(P(("gx", "gz"), None), P("gx", None, "gz", None)),
        check_vma=False,
    )
```

time: 572 us -> 69.2 us (0.12); the launches traced: 560 us -> 68.8 us
  waiting for transfers between devices: 293 us -> 0 us
  local copies, waits for them, and re-layouts: 135 us -> 3.08 us
  starting transfers between devices: 69.6 us -> 0 us
  Pallas kernels: 0 us -> 64.4 us
  other arithmetic: 39.4 us -> 0 us
  between operations: 17.2 us -> 1.3 us
  matrix products: 6.62 us -> 0 us
    all_to_all x5 -> x0, waiting for transfers between devices: 246 us -> none  [the longest x3 215 us: shards(): lax.all_to_all(answers, 'gx', split_axis=0, concat_axis=0, tiled=True)]
    reshape x47 -> x2, local copies, waits for them, and re-layouts: 73.8 us -> 0.65 us  [shards(): part = part.reshape(3, SIDE // n_gz, DENSE, 256)]
    all_to_all x5 -> x0, starting transfers between devices: 69.5 us -> none  [the longest x3 38 us: shards(): lax.all_to_all(answers, 'gx', split_axis=0, concat_axis=0, tiled=True)]
    pallas_call x0 -> x1, Pallas kernels: none -> 64.4 us  [shards(): pl.pallas_call(functools.partial(kernel, n_gx, n_gz), out_shape=(jax.Shap...]
    unnamed x2 -> x0, waiting for transfers between devices: 46.8 us -> none
    gather x24 -> x0, local copies, waits for them, and re-layouts: 26.1 us -> none  [the longest x8 15.1 us: answer(): faces_now[source_row]]
    select_n x26 -> x0, other arithmetic: 24.1 us -> none  [the longest x9 12.4 us: reinit_step(): chosen = jnp.where(to_strips(start, axis_id) > 0.0, outward, inward)]
    transpose x4 -> x0, local copies, waits for them, and re-layouts: 9.86 us -> none  [the longest x3 5.94 us: to_strips(): block_cube = jnp.swapaxes(block_cube, -3, -2)]
  transfers between devices with their start and end apart: 6 -> 0, of which waited for: 6 -> 0; matrix products, arithmetic and copies ran while one was open for 3% -> 0% of each run, Pallas kernels for 0% -> 0%
where the time goes in v1:
time: 69.2 us; the launch traced here: 68.8 us
  Pallas kernels  64.4 us (93%)
  local copies, waits for them, and re-layouts  3.08 us (4%)
  between operations  1.3 us (2%)
    pallas_call x1, Pallas kernels, shards(): pl.pallas_call(functools.partial(kernel, n_gx, n_gz), out_shape=(jax.Shap...  64.4 us
    unnamed x6, local copies, waits for them, and re-layouts  2.43 us

profile of v1, /device:TPU:1, one launch (start us, length us, event | category | flops | bytes accessed | tf_op | source)
XLA Modules:
  0.0 68.8 jit_solution(3068021993882178662)
XLA Ops:
  1.3 0.0 copy-start.1
  1.3 0.8 %copy.6.nb = s32[16,6]{1,0:T(8,128)S(1)} copy(s32[16,6]{0,1:T(8,128)} %param.5) | data formatting | bytes 768 | tf_op args[1]
  2.1 0.0 copy-done.1
  2.1 0.0 copy-start
  2.1 0.9 %copy-done = f32[16,4096]{1,0:T(8,128)S(1)} copy-done((f32[16,4096]{1,0:T(8,128)S(1)}, f32[16,4096]{1,0:T(8,128)}, u32[]{:S(2)}) %copy-start) | copy-done | bytes 262168
  3.0 64.4 %shard_map.59 = (f32[16,4096]{1,0:T(8,128)S(1)}, f32[3,16,256]{2,1,0:T(8,128)S(1)}) custom-call(s32[16,6]{1,0:T(8,128)S(1)} %copy.6.nb, s32[1]{0:T(128)S(6)} %copy.11.live, s32[16]{0:T(128)S(1)} %copy-done.1, f32[16,4096]{1,0:T(8,128)S(1)} %copy-done), custom_call_target="tpu_custom_call" | custom-call | tf_op jit(solution)/shard_map/pallas_call | solution.py:391
  67.4 0.6 copy.9
  68.1 0.7 %copy.12 = f32[16,4096]{1,0:T(8,128)} copy(f32[16,4096]{1,0:T(8,128)S(1)} %get-tuple-element.8) | data formatting | bytes 524288
  (1 shorter events, 0.0 us)
Async XLA Ops:
  1.3 0.8 %copy-start.1 = (s32[16]{0:T(128)S(1)}, s32[16]{0:T(128)}, u32[]{:S(2)}) copy-start(s32[16]{0:T(128)} %target.1) | copy-start | bytes 196
  2.1 1.0 %copy-start = (f32[16,4096]{1,0:T(8,128)S(1)}, f32[16,4096]{1,0:T(8,128)}, u32[]{:S(2)}) copy-start(f32[16,4096]{1,0:T(8,128)} %start.1) | copy-start | bytes 786436

commit v2 on v1

--- a/solution.py
+++ b/solution.py
@@ -16,7 +16,9 @@
 BAND_WIDTH = 1.5
 MESH = pl.DeviceIdType.MESH
 
-PEERS = (0, 1, 2, 4, 5, 6, 7)
+PEERS = (7, 0, 6, 1, 5, 2, 4)
+NEAR = (0, 6, 1, 5, 2, 4)
+FAR = 7
 AXIS_ROWS = 512
 
 
@@ -95,10 +97,10 @@
     return lax.dot_general(a, b, (((1,), (0,)), ((), ())), preferred_element_type=jnp.float32)
 
 
-def kernel(n_gx, n_gz, nb, live, target, start, level_out, part_out,
-           u, faces, ghost, sigma, grad, speed, missing, near_col, far_col, force, request, heard,
+def kernel(n_gx, n_gz, table, live, target, level, level_out, part_out,
+           nb, start, u, faces, ghost, sigma, grad, speed, missing, near_col, far_col, take, far_sigma, force, request, heard,
            sends, recvs, fsend, frecv,
-           request_sent, request_got, sent, got, fsent, fgot):
+           table_loaded, loaded, request_sent, request_got, sent, got, fsent, fgot):
     me = lax.axis_index("gx")
     layer = lax.axis_index("gz")
 
@@ -106,6 +108,10 @@
         step = n_gx // 2 if peer == 7 else peer - 3
         return {"gx": lax.rem(me + step + n_gx, n_gx)}
 
+    load = pltpu.make_async_copy(level, start, loaded)
+    load.start()
+    load_table = pltpu.make_async_copy(table, nb, table_loaded)
+    load_table.start()
     barrier = pltpu.get_barrier_semaphore()
     for peer in PEERS:
         pl.semaphore_signal(barrier, inc=1, device_id=peer_id(peer), device_id_type=MESH)
@@ -114,8 +120,13 @@
 
     square_rows = lax.broadcasted_iota(jnp.int32, (128, 128), 0)
     square_lanes = lax.broadcasted_iota(jnp.int32, (128, 128), 1)
-    entry = [jnp.broadcast_to(nb[:, side:side + 1], (16, 128)) for side in range(6)]
-    entry = jnp.concatenate(entry + [jnp.full((32, 128), -1, jnp.int32)], 0)
+    load_table.wait()
+    spots = [jnp.broadcast_to(nb[side:side + 1, :], (16, 16)) for side in range(6)]
+    spots = jnp.concatenate(spots + [jnp.full((32, 16), -1, jnp.int32)], 0)
+    own_spot = lax.broadcasted_iota(jnp.int32, (128, 16), 0) & 15
+    own_spot = own_spot == lax.broadcasted_iota(jnp.int32, (128, 16), 1)
+    entry = jnp.sum(jnp.where(own_spot, spots, 0).astype(jnp.float32), 1, keepdims=True)
+    entry = jnp.broadcast_to(entry, (128, 128)).astype(jnp.int32)
     held = entry >= 0
     away = (entry >> (SLOTS * n_gz).bit_length() - 1) - me + 3
     kind = jnp.minimum(away & (n_gx - 1), 7)
@@ -128,13 +139,15 @@
     slot = jnp.where(remote, slot, -16.0)
     lane_ids = square_lanes.astype(jnp.float32)
     face = face.astype(jnp.float32)
-    asked = dot_rows(as_one(slot == lane_ids), face.astype(jnp.bfloat16))
+    chosen = as_one(slot == lane_ids)
+    asked = dot_rows(chosen, face.astype(jnp.bfloat16))
     asked = asked + dot_rows(as_one(slot + 4.0 == lane_ids), (face + 128.0).astype(jnp.bfloat16))
     request[...] = asked[:64].reshape(8, 8, 128)
     far_col[...] = slot[:96]
+    take[...] = dot_rows(chosen, as_one(square_rows == square_lanes))[56:64]
     near_col[...] = jnp.where(jnp.logical_and(held, kind == 3), face, -16.0)[:96]
     missing[...] = jnp.where(held, 0.0, 1.0)[:96]
-    faces[96:, :] = jnp.zeros((32, 768), jnp.float32)
+    faces[96:, :] = jnp.zeros((32, 1536), jnp.float32)
 
     pl.semaphore_wait(barrier, len(PEERS) + n_gz - 1)
     for peer in PEERS:
@@ -150,11 +163,11 @@
         return pl.ds(axis * AXIS_ROWS + position * 32 + tile * 16, 16)
 
     def keep_face(axis, position, tile, value):
-        if 3 <= position < 13:
-            return
-        side = 2 * axis + (position >= 13)
-        at = ((position % 13) * 2 + tile) * 128
-        faces[side * 16:side * 16 + 16, at:at + 128] = value
+        depth = min(position, 15 - position)
+        if depth < 6:
+            side = 2 * axis + (position >= 8)
+            at = (depth * 2 + tile) * 128
+            faces[side * 16:side * 16 + 16, at:at + 128] = value
 
     def spread(tile, x_of):
         ys = []
@@ -169,6 +182,7 @@
             keep_face(2, z, tile, zs[z])
         return ys, zs
 
+    load.wait()
     for tile in range(2):
         tops = {}
         for i in range(8):
@@ -198,7 +212,7 @@
             device_id=peer_id(peer), device_id_type=MESH)
 
     def serve(turn):
-        hi, mid, low = split3(faces[...])
+        hi, mid, low = split3(faces[:, :768])
         cols = heard[...].reshape(64, 128)
         left = as_one(cols == lane_ids[:64])
         right = as_one(cols == lane_ids[:64] + 128.0)
@@ -218,11 +232,11 @@
                 at = (side * 6 + part) * 16
                 ghost[at:at + 16, :] = out[side * 16:side * 16 + 16, part * 128:part * 128 + 128]
 
-    def fetch(turn):
-        for peer in PEERS:
+    def fetch_near(turn):
+        for peer in NEAR:
             copy_of(turn, peer, peer).wait()
-        hi, mid, low = split3(jnp.concatenate([recvs[turn, c] if c in PEERS else jnp.zeros((8, 384), jnp.float32)
-                                               for c in range(8)], 0))
+        none = jnp.zeros((8, 384), jnp.float32)
+        hi, mid, low = split3(jnp.concatenate([recvs[turn, c] if c in NEAR else none for c in range(8)], 0))
         arrived = jnp.concatenate([hi, mid, low, jnp.zeros_like(low)], 0)
         fold = jnp.where(lane_ids[:96] >= 64.0, lane_ids[:96] - 64.0, lane_ids[:96])
         for half in range(2):
@@ -233,11 +247,50 @@
                     at = (side * 6 + half * 3 + part) * 16
                     ghost[at:at + 16, :] += out[side * 16:side * 16 + 16, part * 128:part * 128 + 128]
 
+    def own_cells():
+        hi, mid, low = split3(faces[...])
+        one = take[...].astype(jnp.bfloat16)
+        return dot(jnp.concatenate([one, one], 1), jnp.concatenate([hi, mid], 0)) + dot(one, low)
+
+    def put_far(values):
+        parts = [part.astype(jnp.float32) for part in split3(values)]
+        parts = jnp.concatenate(parts + [jnp.zeros_like(values)], 0).astype(jnp.bfloat16)
+        lanes = lax.broadcasted_iota(jnp.int32, (96, 32), 1)
+        rows = jnp.where(lanes < 24, (lanes & 7) + 56, -1).astype(jnp.float32)
+        return dot(as_one(far_col[:, :32] == rows), parts)
+
+    def is_far(side):
+        return far_col[side * 16:side * 16 + 16, :] >= 56.0
+
+    def far_weno(turn, own):
+        copy_of(turn, FAR, FAR).wait()
+        came = recvs[turn, FAR]
+        other = pltpu.roll(came, 4, 0)
+        result = {}
+        for tile in range(2):
+            values = {}
+            for depth in range(3):
+                part = depth * 2 + tile
+                from_ = came if part < 3 else other
+                values[-1 - depth] = from_[:, part % 3 * 128:part % 3 * 128 + 128]
+            for depth in range(6):
+                at = (depth * 2 + tile) * 128
+                values[depth] = own[:, at:at + 128]
+
+            def signs(i):
+                return far_sigma[:, (i * 2 + tile) * 128:(i * 2 + tile) * 128 + 128]
+
+            def store(i, value):
+                result[i * 2 + tile] = value
+
+            weno_axis(values, 0, 3, signs, store)
+        return put_far(jnp.concatenate([result[part] for part in range(6)], 1))
+
     def column_rows(axis, position, column):
         return pl.ds(axis * AXIS_ROWS + position * 32 + column * 8, 8)
 
-    def ghosts_at(axis, high, layer_id, column, edge):
-        values = ghost[pl.ds((2 * axis + high) * 96 + layer_id * 32 + column * 8, 8), :]
+    def ghosts_at(axis, high, depth, column, edge):
+        values = ghost[pl.ds((2 * axis + high) * 96 + depth * 32 + column * 8, 8), :]
         gone = missing[pl.ds((2 * axis + high) * 16 + (column % 2) * 8, 8), :]
         return jnp.where(gone > 0.0, edge, values)
 
@@ -255,13 +308,16 @@
             return
         values = {i: load(i) for i in range(6)}
         for i in range(3):
-            values[i - 3] = ghosts_at(axis, 0, i, column, values[0])
+            values[-1 - i] = ghosts_at(axis, 0, i, column, values[0])
         weno_axis(values, 0, 3, signs, store)
         values = {i: load(i) for i in range(10, 16)}
         for i in range(3):
             values[16 + i] = ghosts_at(axis, 1, i, column, values[15])
         weno_axis(values, 13, 16, signs, store)
 
+    first = own_cells()[:, :768]
+    far_sigma[...] = jnp.where(first > 0.0, 1.0, -1.0)
+
     def step(turn, carry):
         serve(turn)
 
@@ -274,18 +330,29 @@
             return c
 
         lax.fori_loop(0, 12, inner, 0)
-        fetch(turn)
+        own = own_cells()
+        fetch_near(turn)
         lax.fori_loop(0, 12, outer, 0)
+        fixed = far_weno(turn, own)
+
+        def grad_at(axis, position, tile):
+            value = grad[rows_of(axis, position, tile), :]
+            depth = min(position, 15 - position)
+            if depth >= 3:
+                return value
+            side = 2 * axis + (position >= 8)
+            at = (depth * 2 + tile) * 128
+            return jnp.where(is_far(side), fixed[side * 16:side * 16 + 16, at:at + 128], value)
 
         for tile in range(2):
-            sums = exchange([grad[rows_of(2, z, tile), :] for z in range(16)], 1, fine_masks)
-            sums = [sums[y] + grad[rows_of(1, y, tile), :] for y in range(16)]
+            sums = exchange([grad_at(2, z, tile) for z in range(16)], 1, fine_masks)
+            sums = [sums[y] + grad_at(1, y, tile) for y in range(16)]
             fresh = {}
             for ytile in range(2):
                 xs = exchange(sums[ytile * 8:ytile * 8 + 8], 16, coarse_masks)
                 for i in range(8):
                     rows = rows_of(0, tile * 8 + i, ytile)
-                    steep = jnp.sqrt(xs[i] + grad[rows, :])
+                    steep = jnp.sqrt(xs[i] + grad_at(0, tile * 8 + i, ytile))
                     value = u[rows, :] - speed[rows, :] * (steep - 3.0)
                     u[rows, :] = value
                     keep_face(0, tile * 8 + i, ytile, value)
@@ -301,11 +368,15 @@
         for ytile in range(2):
             at = x * 256 + ytile * 128
             level_out[:, at:at + 128] = jnp.where(keep, u[rows_of(0, x, ytile), :], 0.0)
-    fetch(STEPS)
+    fetch_near(STEPS)
+    copy_of(STEPS, FAR, FAR).wait()
+    far_rim = put_far(recvs[STEPS, FAR, :, :256])
 
     def rim(axis, high, tile, edge):
-        values = ghost[pl.ds((2 * axis + high) * 96 + (2 - 2 * high) * 32 + tile * 16, 16), :]
-        return jnp.where(missing[pl.ds((2 * axis + high) * 16, 16), :] > 0.0, edge, values)
+        side = 2 * axis + high
+        values = ghost[side * 96 + tile * 16:side * 96 + tile * 16 + 16, :]
+        values = jnp.where(is_far(side), far_rim[side * 16:side * 16 + 16, tile * 128:tile * 128 + 128], values)
+        return jnp.where(missing[side * 16:side * 16 + 16, :] > 0.0, edge, values)
 
     def beside(axis, position, tile):
         here = u[rows_of(axis, position, tile), :]
@@ -387,15 +458,18 @@
     share = 64 // n_gz
     smem = pl.BlockSpec(memory_space=pltpu.SMEM)
     vmem = pl.BlockSpec(memory_space=pltpu.VMEM)
+    hbm = pl.BlockSpec(memory_space=pltpu.HBM)
     dma, f32 = pltpu.SemaphoreType.DMA, jnp.float32
     level, part = pl.pallas_call(
         functools.partial(kernel, n_gx, n_gz),
         out_shape=(jax.ShapeDtypeStruct(level_set.shape, f32), jax.ShapeDtypeStruct((3, share, 256), f32)),
-        in_specs=[vmem, smem, smem, vmem],
+        in_specs=[hbm, smem, smem, hbm],
         out_specs=(vmem, vmem),
         scratch_shapes=[
+            pltpu.VMEM((6, SLOTS), jnp.int32),
+            pltpu.VMEM(level_set.shape, f32),
             pltpu.VMEM((3 * AXIS_ROWS, 128), f32),
-            pltpu.VMEM((128, 768), f32),
+            pltpu.VMEM((128, 1536), f32),
             pltpu.VMEM((36 * 16, 128), f32),
             pltpu.VMEM((3 * AXIS_ROWS, 128), f32),
             pltpu.VMEM((3 * AXIS_ROWS, 128), f32),
@@ -403,6 +477,8 @@
             pltpu.VMEM((96, 128), f32),
             pltpu.VMEM((96, 128), f32),
             pltpu.VMEM((96, 128), f32),
+            pltpu.VMEM((8, 128), f32),
+            pltpu.VMEM((8, 768), f32),
             pltpu.VMEM((3, 128, 256), f32),
             pltpu.VMEM((8, 8, 128), f32),
             pltpu.VMEM((8, 8, 128), f32),
@@ -410,11 +486,11 @@
             pltpu.VMEM((ROUNDS, 8, 8, 384), f32),
             pltpu.VMEM((n_gz, 3, share, 256), f32),
             pltpu.VMEM((n_gz - 1, 3, share, 256), f32),
-            dma((8,)), dma((8,)), dma((ROUNDS, 8)), dma((ROUNDS, 8)), dma((n_gz - 1,)), dma((n_gz - 1,)),
+            dma(()), dma(()), dma((8,)), dma((8,)), dma((ROUNDS, 8)), dma((ROUNDS, 8)), dma((n_gz - 1,)), dma((n_gz - 1,)),
         ],
         compiler_params=pltpu.CompilerParams(
-            collective_id=0, has_side_effects=True, vmem_limit_bytes=24 << 20),
-    )(neighbours, live_count, dense_target, level_set)
+            collective_id=0, has_side_effects=True, vmem_limit_bytes=60 << 20),
+    )(neighbours.T, live_count, dense_target, level_set)
     part = part.reshape(3, SIDE // n_gz, DENSE, 256)
     return level, jnp.transpose(part, (2, 0, 1, 3))
 

time: 69.2 us -> 66.9 us (0.967)
  Pallas kernels: 64.4 us -> 61.9 us
    pallas_call x1, Pallas kernels: 64.4 us -> 61.9 us  [shards(): pl.pallas_call(functools.partial(kernel, n_gx, n_gz), out_shape=(jax.Shap...]
    reshape x2, local copies, waits for them, and re-layouts: 0.65 us -> 1.45 us  [shards(): part = part.reshape(3, SIDE // n_gz, DENSE, 256)]
    unnamed x6 -> x1, local copies, waits for them, and re-layouts: 2.43 us -> 1.67 us
where the time goes in v2:
time: 66.9 us; the launch traced here: 66.3 us
  Pallas kernels  61.9 us (93%)
  local copies, waits for them, and re-layouts  3.12 us (5%)
  between operations  1.29 us (2%)
    pallas_call x1, Pallas kernels, shards(): pl.pallas_call(functools.partial(kernel, n_gx, n_gz), out_shape=(jax.Shap...  61.9 us
    unnamed x1, local copies, waits for them, and re-layouts  1.67 us
    reshape x2, local copies, waits for them, and re-layouts, shards(): part = part.reshape(3, SIDE // n_gz, DENSE, 256)  1.45 us

profile of v2, /device:TPU:1, one launch (start us, length us, event | category | flops | bytes accessed | tf_op | source)
XLA Modules:
  0.0 66.3 jit_solution(9011532092205738337)
XLA Ops:
  1.3 61.9 %shard_map.59 = (f32[16,4096]{1,0:T(8,128)}, f32[3,16,256]{2,1,0:T(8,128)}) custom-call(s32[6,16]{1,0:T(8,128)} %bitcast.5, s32[1]{0:T(128)S(6)} %copy.10.live, s32[16]{0:T(128)} %target.1, f32[16,4096]{1,0:T(8,128)} %level.1), custom_call_target="tpu_custom_call" | custom-call | tf_op jit(solution)/shard_map/pallas_call | solution.py:463
  63.1 0.8 %reshape.7 = f32[3,4,4,256]{3,2,1,0:T(4,128)S(1)} reshape(f32[3,16,256]{2,1,0:T(8,128)} %get-tuple-element.5) | data formatting | bytes 98304 | tf_op jit(solution)/shard_map/reshape | solution.py:494
  64.0 0.6 copy.8
  64.6 1.7 %copy.11 = f32[16,4096]{1,0:T(8,128)} copy(f32[16,4096]{1,0:T(8,128)} %get-tuple-element.8) | data formatting | bytes 524288

commit v3 on v2

--- a/solution.py
+++ b/solution.py
@@ -97,10 +97,10 @@
     return lax.dot_general(a, b, (((1,), (0,)), ((), ())), preferred_element_type=jnp.float32)
 
 
-def kernel(n_gx, n_gz, table, live, target, level, level_out, part_out,
-           nb, start, u, faces, ghost, sigma, grad, speed, missing, near_col, far_col, take, far_sigma, force, request, heard,
+def kernel(n_gx, n_gz, table, live, target_in, level, level_out, part_out,
+           nb, target, start, u, faces, ghost, sigma, grad, speed, missing, near_col, far_col, take, far_sigma, force, request, heard,
            sends, recvs, fsend, frecv,
-           table_loaded, loaded, request_sent, request_got, sent, got, fsent, fgot):
+           table_loaded, target_loaded, loaded, request_sent, request_got, sent, got, fsent, fgot):
     me = lax.axis_index("gx")
     layer = lax.axis_index("gz")
 
@@ -112,6 +112,8 @@
     load.start()
     load_table = pltpu.make_async_copy(table, nb, table_loaded)
     load_table.start()
+    load_target = pltpu.make_async_copy(target_in, target, target_loaded)
+    load_target.start()
     barrier = pltpu.get_barrier_semaphore()
     for peer in PEERS:
         pl.semaphore_signal(barrier, inc=1, device_id=peer_id(peer), device_id_type=MESH)
@@ -182,6 +184,7 @@
             keep_face(2, z, tile, zs[z])
         return ys, zs
 
+    load_target.wait()
     load.wait()
     for tile in range(2):
         tops = {}
@@ -429,6 +432,15 @@
     pick = jnp.logical_and(pick, (lane_bricks >> 4) == ((out_rows >> 2) & 7))
     pick = jnp.where(pick, 1.0, 0.0).astype(jnp.bfloat16)
     share = 64 // n_gz
+    turns = sorted(range(1, n_gz), key=lambda turn: abs(2 * turn - n_gz))
+
+    def part_copy(a, turn):
+        to = lax.rem(layer + turn, n_gz)
+        return pltpu.make_async_remote_copy(
+            src_ref=fsend.at[to, a], dst_ref=frecv.at[turn - 1, a],
+            send_sem=fsent.at[turn - 1, a], recv_sem=fgot.at[turn - 1, a],
+            device_id={"gz": to}, device_id_type=MESH)
+
     for a in range(3):
         hi, mid, low = split3(force[a])
         block = dot(hi, average) + (dot(mid, average) + dot(low, average))
@@ -437,36 +449,32 @@
         result = dot(pick, hi) + (dot(pick, mid) + dot(pick, low))
         for g in range(n_gz):
             fsend[g, a] = result[g * share:(g + 1) * share]
-
-    def part_copy(turn):
-        to = lax.rem(layer + turn, n_gz)
-        return pltpu.make_async_remote_copy(
-            src_ref=fsend.at[to], dst_ref=frecv.at[turn - 1],
-            send_sem=fsent.at[turn - 1], recv_sem=fgot.at[turn - 1],
-            device_id={"gz": to}, device_id_type=MESH)
-
-    for turn in range(1, n_gz):
-        part_copy(turn).start()
-    total = fsend[layer]
-    for turn in range(1, n_gz):
-        part_copy(turn).wait()
-        total = total + frecv[turn - 1]
-    part_out[...] = total
+        for turn in turns:
+            part_copy(a, turn).start()
+    for a in range(3):
+        total = fsend[layer, a]
+        for turn in turns:
+            part_copy(a, turn).wait()
+            total = total + frecv[turn - 1, a]
+        part_out[a] = total
 
 
 def shards(n_gx, n_gz, level_set, neighbours, live_count, dense_target):
     share = 64 // n_gz
-    smem = pl.BlockSpec(memory_space=pltpu.SMEM)
     vmem = pl.BlockSpec(memory_space=pltpu.VMEM)
-    hbm = pl.BlockSpec(memory_space=pltpu.HBM)
+    anywhere = pl.BlockSpec(memory_space=pl.ANY)
     dma, f32 = pltpu.SemaphoreType.DMA, jnp.float32
+    def far_memory(array):
+        return pltpu.with_memory_space_constraint(array, pltpu.HBM)
+
     level, part = pl.pallas_call(
         functools.partial(kernel, n_gx, n_gz),
         out_shape=(jax.ShapeDtypeStruct(level_set.shape, f32), jax.ShapeDtypeStruct((3, share, 256), f32)),
-        in_specs=[hbm, smem, smem, hbm],
+        in_specs=[anywhere, pl.BlockSpec(memory_space=pltpu.SMEM), anywhere, anywhere],
         out_specs=(vmem, vmem),
         scratch_shapes=[
             pltpu.VMEM((6, SLOTS), jnp.int32),
+            pltpu.SMEM((SLOTS,), jnp.int32),
             pltpu.VMEM(level_set.shape, f32),
             pltpu.VMEM((3 * AXIS_ROWS, 128), f32),
             pltpu.VMEM((128, 1536), f32),
@@ -486,11 +494,11 @@
             pltpu.VMEM((ROUNDS, 8, 8, 384), f32),
             pltpu.VMEM((n_gz, 3, share, 256), f32),
             pltpu.VMEM((n_gz - 1, 3, share, 256), f32),
-            dma(()), dma(()), dma((8,)), dma((8,)), dma((ROUNDS, 8)), dma((ROUNDS, 8)), dma((n_gz - 1,)), dma((n_gz - 1,)),
+            dma(()), dma(()), dma(()), dma((8,)), dma((8,)), dma((ROUNDS, 8)), dma((ROUNDS, 8)), dma((n_gz - 1, 3)), dma((n_gz - 1, 3)),
         ],
         compiler_params=pltpu.CompilerParams(
-            collective_id=0, has_side_effects=True, vmem_limit_bytes=60 << 20),
-    )(neighbours.T, live_count, dense_target, level_set)
+            collective_id=0, has_side_effects=True, vmem_limit_bytes=24 << 20),
+    )(far_memory(neighbours.T), live_count, far_memory(dense_target), far_memory(level_set))
     part = part.reshape(3, SIDE // n_gz, DENSE, 256)
     return level, jnp.transpose(part, (2, 0, 1, 3))
 

time: 66.9 us -> 63.4 us (0.948)
  Pallas kernels: 61.9 us -> 60.1 us
  local copies, waits for them, and re-layouts: 3.12 us -> 1.35 us
    pallas_call x1, Pallas kernels: 61.9 us -> 60.1 us  [shards(): pl.pallas_call(functools.partial(kernel, n_gx, n_gz), out_shape=(jax.Shap...]
    unnamed x1, local copies, waits for them, and re-layouts: 1.67 us -> 0.7 us
    reshape x2, local copies, waits for them, and re-layouts: 1.45 us -> 0.65 us  [shards(): part = part.reshape(3, SIDE // n_gz, DENSE, 256)]
where the time goes in v3:
time: 63.4 us; the launch traced here: 62.7 us
  Pallas kernels  60.1 us (95%)
  local copies, waits for them, and re-layouts  1.35 us (2%)
  between operations  1.29 us (2%)
    pallas_call x1, Pallas kernels, shards(): pl.pallas_call(functools.partial(kernel, n_gx, n_gz), out_shape=(jax.Shap...  60.1 us

profile of v3, /device:TPU:1, one launch (start us, length us, event | category | flops | bytes accessed | tf_op | source)
XLA Modules:
  0.0 62.7 jit_solution(14746262222710448417)
XLA Ops:
  1.3 60.1 %shard_map.59 = (f32[16,4096]{1,0:T(8,128)S(1)}, f32[3,16,256]{2,1,0:T(8,128)S(1)}) custom-call(s32[6,16]{1,0:T(8,128)} %bitcast.5, s32[1]{0:T(128)S(6)} %copy.10.live, s32[16]{0:T(128)} %target_in.1, f32[16,4096]{1,0:T(8,128)} %level.1), custom_call_target="tpu_custom_call" | custom-call | tf_op jit(solution)/shard_map/pallas_call | solution.py:470
  61.4 0.6 %copy.8 = f32[3,4,4,256]{3,1,0,2:T(4,128)} copy(f32[3,4,4,256]{3,2,1,0:T(4,128)S(1)} %reshape.7) | data formatting | bytes 98304 | tf_op jit(solution)/shard_map/reshape | solution.py:502
  62.0 0.7 %copy.11 = f32[16,4096]{1,0:T(8,128)} copy(f32[16,4096]{1,0:T(8,128)S(1)} %get-tuple-element.8) | data formatting | bytes 524288
  (1 shorter events, 0.0 us)

commit v4 on v3

--- a/solution.py
+++ b/solution.py
@@ -371,14 +371,36 @@
         for ytile in range(2):
             at = x * 256 + ytile * 128
             level_out[:, at:at + 128] = jnp.where(keep, u[rows_of(0, x, ytile), :], 0.0)
+
+    r = lax.broadcasted_iota(jnp.int32, (256, 256), 0)
+    l = lax.broadcasted_iota(jnp.int32, (256, 256), 1)
+    same = jnp.logical_and((r >> 5) == ((l >> 4) & 7), ((r >> 1) & 7) == (l & 7))
+    average = jnp.where(same, 1.0 / 16.0, 0.0).astype(jnp.bfloat16)
+    average = jnp.concatenate([average, average], 0)
+    swap = as_one(l == (r & 15) * 16 + (r >> 4))
+    swap = jnp.concatenate([swap, swap, swap], 0)
+    lanes = lax.broadcasted_iota(jnp.int32, (16, 256), 1)
+    brick_rows = lax.broadcasted_iota(jnp.int32, (16, 256), 0)
+    lane_bricks = lax.broadcasted_iota(jnp.int32, (64, 128), 1)
+    by_row = jnp.zeros((16, 256), jnp.int32)
+    by_lane = jnp.full((64, 128), -1, jnp.int32)
+    for b in range(16):
+        by_row = jnp.where(brick_rows == b, target[b], by_row)
+        by_lane = jnp.where((lane_bricks & 15) == b, target[b], by_lane)
+    octant = jnp.logical_and(((by_row >> 2) & 1) == (lanes >> 7), ((by_row >> 1) & 1) == ((lanes >> 3) & 1))
+    octant = jnp.where(octant, 1.0, 0.0)
+    share, deep = 64 // n_gz, SIDE // n_gz
+    out_rows = lax.broadcasted_iota(jnp.int32, (64, 128), 0)
+    out_z = (out_rows // share) * deep + (out_rows & (deep - 1))
+    pick = jnp.logical_and((by_lane >> 3) == (out_rows & (share - 1)) // deep, (by_lane & 1) == (out_z >> 3))
+    pick = as_one(jnp.logical_and(pick, (lane_bricks >> 4) == (out_z & 7)))
+    turns = sorted(range(1, n_gz), key=lambda turn: abs(2 * turn - n_gz))
+
     fetch_near(STEPS)
-    copy_of(STEPS, FAR, FAR).wait()
-    far_rim = put_far(recvs[STEPS, FAR, :, :256])
 
     def rim(axis, high, tile, edge):
         side = 2 * axis + high
         values = ghost[side * 96 + tile * 16:side * 96 + tile * 16 + 16, :]
-        values = jnp.where(is_far(side), far_rim[side * 16:side * 16 + 16, tile * 128:tile * 128 + 128], values)
         return jnp.where(missing[side * 16:side * 16 + 16, :] > 0.0, edge, values)
 
     def beside(axis, position, tile):
@@ -397,42 +419,53 @@
         laps = exchange([lap_y[y] + parts[y][0] for y in range(16)], 1, fine_masks)
         grad_x = exchange(grad_x, 1, fine_masks)
         grad_y = exchange([p[1] for p in parts], 1, fine_masks)
-        held = None
         for z in range(16):
             lap, grad_z, here = beside(2, z, tile)
-            lap = lap + laps[z]
             v2 = jnp.minimum(here * here, BAND_WIDTH * BAND_WIDTH) * ((math.pi / 3.0) ** 2)
             wave = 1.0 / 479001600.0
             for power in (-1.0 / 3628800.0, 1.0 / 40320.0, -1.0 / 720.0, 1.0 / 24.0, -0.5, 1.0):
                 wave = wave * v2 + power
-            lap = jnp.where(jnp.abs(here) < BAND_WIDTH, lap * (wave * wave * (2.0 / 3.0)), 0.0)
-            forces = [lap * grad_x[z], lap * grad_y[z], lap * grad_z]
+            grad[rows_of(0, z, tile), :] = lap + laps[z]
+            grad[rows_of(1, z, tile), :] = grad_x[z]
+            grad[rows_of(2, z, tile), :] = grad_y[z]
+            sigma[rows_of(0, z, tile), :] = grad_z
+            sigma[rows_of(1, z, tile), :] = jnp.where(jnp.abs(here) < BAND_WIDTH, wave * wave * (2.0 / 3.0), 0.0)
+
+    copy_of(STEPS, FAR, FAR).wait()
+    far_rim = put_far(recvs[STEPS, FAR, :, :256])
+    turned = dot(jnp.concatenate(split3(far_rim[:32]), 1), swap)
+    groups = lax.broadcasted_iota(jnp.int32, (16, 128), 1)
+    y_ids, x_ids = groups & 15, groups >> 4
+
+    def moved_to(mask, values, by):
+        return jnp.where(mask, pltpu.roll(values, by % 128, 1) if by % 128 else values, 0.0)
+
+    for tile in range(2):
+        edge = 7 * tile
+        held = None
+        for z in range(16):
+            at = z // 8 * 128
+            add_x = moved_to(x_ids == edge, turned[tile * 16:tile * 16 + 16, at:at + 128], 16 * (edge - z % 8))
+            at = tile * 128
+            low_y = moved_to(y_ids == 0, far_rim[32:48, at:at + 128], -z)
+            high_y = moved_to(y_ids == 15, far_rim[48:64, at:at + 128], 15 - z)
+            lap = (grad[rows_of(0, z, tile), :] + add_x) + (low_y + high_y)
+            grad_x = grad[rows_of(1, z, tile), :] + (add_x if tile else -add_x)
+            grad_y = grad[rows_of(2, z, tile), :] + (high_y - low_y)
+            grad_z = sigma[rows_of(0, z, tile), :]
+            if z == 0:
+                lap = lap + far_rim[64:80, at:at + 128]
+                grad_z = grad_z - far_rim[64:80, at:at + 128]
+            if z == 15:
+                lap = lap + far_rim[80:96, at:at + 128]
+                grad_z = grad_z + far_rim[80:96, at:at + 128]
+            lap = lap * sigma[rows_of(1, z, tile), :]
+            forces = [lap * grad_x, lap * grad_y, lap * grad_z]
             if z % 2 == 0:
                 held = forces
             else:
                 for a in range(3):
-                    force[a, pl.ds(z // 2 * 16, 16), tile * 128:tile * 128 + 128] = held[a] + forces[a]
-
-    r = lax.broadcasted_iota(jnp.int32, (256, 256), 0)
-    l = lax.broadcasted_iota(jnp.int32, (256, 256), 1)
-    same = jnp.logical_and((r >> 5) == ((l >> 4) & 7), ((r >> 1) & 7) == (l & 7))
-    average = jnp.where(same, 1.0 / 16.0, 0.0).astype(jnp.bfloat16)
-    lanes = lax.broadcasted_iota(jnp.int32, (16, 256), 1)
-    brick_rows = lax.broadcasted_iota(jnp.int32, (16, 256), 0)
-    lane_bricks = lax.broadcasted_iota(jnp.int32, (64, 128), 1)
-    by_row = jnp.zeros((16, 256), jnp.int32)
-    by_lane = jnp.full((64, 128), -1, jnp.int32)
-    for b in range(16):
-        by_row = jnp.where(brick_rows == b, target[b], by_row)
-        by_lane = jnp.where((lane_bricks & 15) == b, target[b], by_lane)
-    octant = jnp.logical_and(((by_row >> 2) & 1) == (lanes >> 7), ((by_row >> 1) & 1) == ((lanes >> 3) & 1))
-    octant = jnp.where(octant, 1.0, 0.0)
-    out_rows = lax.broadcasted_iota(jnp.int32, (64, 128), 0)
-    pick = jnp.logical_and((by_lane >> 3) == (out_rows & 3), (by_lane & 1) == (out_rows >> 5))
-    pick = jnp.logical_and(pick, (lane_bricks >> 4) == ((out_rows >> 2) & 7))
-    pick = jnp.where(pick, 1.0, 0.0).astype(jnp.bfloat16)
-    share = 64 // n_gz
-    turns = sorted(range(1, n_gz), key=lambda turn: abs(2 * turn - n_gz))
+                    force[a, pl.ds(z // 2 * 16, 16), at:at + 128] = held[a] + forces[a]
 
     def part_copy(a, turn):
         to = lax.rem(layer + turn, n_gz)
@@ -442,11 +475,10 @@
             device_id={"gz": to}, device_id_type=MESH)
 
     for a in range(3):
-        hi, mid, low = split3(force[a])
-        block = dot(hi, average) + (dot(mid, average) + dot(low, average))
+        block = dot(jnp.concatenate(split3(force[a])[:2], 1), average)
         block = (block.reshape(8, 16, 256) * octant[None]).reshape(128, 256)
-        hi, mid, low = split3(block)
-        result = dot(pick, hi) + (dot(pick, mid) + dot(pick, low))
+        hi, mid, _ = split3(block)
+        result = dot(pick, hi) + dot(pick, mid)
         for g in range(n_gz):
             fsend[g, a] = result[g * share:(g + 1) * share]
         for turn in turns:
@@ -456,7 +488,17 @@
         for turn in turns:
             part_copy(a, turn).wait()
             total = total + frecv[turn - 1, a]
-        part_out[a] = total
+        for s in range(DENSE):
+            part_out[s, a] = total[s * deep:(s + 1) * deep]
+
+
+def finish(level, force, level_out, force_out, level_sem, force_sem):
+    level_copy = pltpu.make_async_copy(level, level_out, level_sem)
+    force_copy = pltpu.make_async_copy(force, force_out, force_sem)
+    level_copy.start()
+    force_copy.start()
+    force_copy.wait()
+    level_copy.wait()
 
 
 def shards(n_gx, n_gz, level_set, neighbours, live_count, dense_target):
@@ -469,7 +511,7 @@
 
     level, part = pl.pallas_call(
         functools.partial(kernel, n_gx, n_gz),
-        out_shape=(jax.ShapeDtypeStruct(level_set.shape, f32), jax.ShapeDtypeStruct((3, share, 256), f32)),
+        out_shape=(jax.ShapeDtypeStruct(level_set.shape, f32), jax.ShapeDtypeStruct((DENSE, 3, SIDE // n_gz, 256), f32)),
         in_specs=[anywhere, pl.BlockSpec(memory_space=pltpu.SMEM), anywhere, anywhere],
         out_specs=(vmem, vmem),
         scratch_shapes=[
@@ -499,8 +541,14 @@
         compiler_params=pltpu.CompilerParams(
             collective_id=0, has_side_effects=True, vmem_limit_bytes=24 << 20),
     )(far_memory(neighbours.T), live_count, far_memory(dense_target), far_memory(level_set))
-    part = part.reshape(3, SIDE // n_gz, DENSE, 256)
-    return level, jnp.transpose(part, (2, 0, 1, 3))
+    results = (level, part)
+    return pl.pallas_call(
+        finish,
+        out_shape=tuple(jax.ShapeDtypeStruct(r.shape, f32) for r in results),
+        in_specs=[anywhere] * 2,
+        out_specs=(anywhere,) * 2,
+        scratch_shapes=[dma(()), dma(())],
+    )(*results)
 
 
 def solution(mesh):

time: 63.4 us -> 75.1 us (1.18)
  Pallas kernels: 60.1 us -> 72.4 us
    pallas_call x0 -> x1, Pallas kernels: none -> 10.5 us  [shards(): pl.pallas_call(finish, out_shape=tuple((jax.ShapeDtypeStruct(r.shape, f32...]
    pallas_call x1, Pallas kernels: 60.1 us -> 61.9 us  [shards(): pl.pallas_call(functools.partial(kernel, n_gx, n_gz), out_shape=(jax.Shap...]
where the time goes in v4:
time: 75.1 us; the launch traced here: 75 us
  Pallas kernels  72.4 us (96%)
  local copies, waits for them, and re-layouts  1.31 us (2%)
  between operations  1.29 us (2%)
    pallas_call x1, Pallas kernels, shards(): pl.pallas_call(functools.partial(kernel, n_gx, n_gz), out_shape=(jax.Shap...  61.9 us
    pallas_call x1, Pallas kernels, shards(): pl.pallas_call(finish, out_shape=tuple((jax.ShapeDtypeStruct(r.shape, f32...  10.5 us

profile of v4, /device:TPU:1, one launch (start us, length us, event | category | flops | bytes accessed | tf_op | source)
XLA Modules:
  0.0 75.0 jit_solution(16724167789328840503)
XLA Ops:
  1.3 61.9 %shard_map.59 = (f32[16,4096]{1,0:T(8,128)S(1)}, f32[4,3,4,256]{3,2,1,0:T(4,128)S(1)}) custom-call(s32[6,16]{1,0:T(8,128)} %bitcast.1, s32[1]{0:T(128)S(6)} %copy.6.live, s32[16]{0:T(128)} %target_in.1, f32[16,4096]{1,0:T(8,128)} %level.1), custom_call_target="tpu_custom_call" | custom-call | tf_op jit(solution)/shard_map/pallas_call | solution.py:512
  63.1 0.0 copy-start
  63.2 0.7 copy-done
  63.8 0.0 copy-start.1
  63.8 0.6 copy-done.1
  64.5 10.5 %shard_map.60 = (f32[16,4096]{1,0:T(8,128)}, f32[4,3,4,256]{3,2,1,0:T(4,128)}) custom-call(f32[16,4096]{1,0:T(8,128)} %copy-done, f32[4,3,4,256]{3,2,1,0:T(4,128)} %copy-done.1), custom_call_target="tpu_custom_call" | custom-call | tf_op jit(solution)/shard_map/pallas_call | solution.py:545
Async XLA Ops:
  63.1 0.7 copy-start
  63.8 0.6 copy-start.1

commit v5 on v4

--- a/solution.py
+++ b/solution.py
@@ -541,7 +541,7 @@
         compiler_params=pltpu.CompilerParams(
             collective_id=0, has_side_effects=True, vmem_limit_bytes=24 << 20),
     )(far_memory(neighbours.T), live_count, far_memory(dense_target), far_memory(level_set))
-    results = (level, part)
+    results = tuple(pltpu.with_memory_space_constraint(r, pltpu.VMEM) for r in (level, part))
     return pl.pallas_call(
         finish,
         out_shape=tuple(jax.ShapeDtypeStruct(r.shape, f32) for r in results),

time: 75.1 us -> 64 us (0.85)
  Pallas kernels: 72.4 us -> 62.6 us
  local copies, waits for them, and re-layouts: 1.31 us -> 0 us
    pallas_call x1, Pallas kernels: 10.5 us -> 0.73 us  [shards(): pl.pallas_call(finish, out_shape=tuple((jax.ShapeDtypeStruct(r.shape, f32...]
    unnamed x4 -> x0, local copies, waits for them, and re-layouts: 1.31 us -> none
where the time goes in v5:
time: 64 us; the launch traced here: 63.9 us
  Pallas kernels  62.6 us (98%)
  between operations  1.28 us (2%)
    pallas_call x1, Pallas kernels, shards(): pl.pallas_call(functools.partial(kernel, n_gx, n_gz), out_shape=(jax.Shap...  61.9 us

profile of v5, /device:TPU:1, one launch (start us, length us, event | category | flops | bytes accessed | tf_op | source)
XLA Modules:
  0.0 63.9 jit_solution(1818816624195810753)
XLA Ops:
  1.3 61.9 %shard_map.59 = (f32[16,4096]{1,0:T(8,128)S(1)}, f32[4,3,4,256]{3,2,1,0:T(4,128)S(1)}) custom-call(s32[6,16]{1,0:T(8,128)} %bitcast.1, s32[1]{0:T(128)S(6)} %copy.6.live, s32[16]{0:T(128)} %target_in.1, f32[16,4096]{1,0:T(8,128)} %level.1), custom_call_target="tpu_custom_call" | custom-call | tf_op jit(solution)/shard_map/pallas_call | solution.py:512
  63.1 0.7 %shard_map.60 = (f32[16,4096]{1,0:T(8,128)}, f32[4,3,4,256]{3,2,1,0:T(4,128)}) custom-call(f32[16,4096]{1,0:T(8,128)S(1)} %get-tuple-element.4.level, f32[4,3,4,256]{3,2,1,0:T(4,128)S(1)} %get-tuple-element.5.force), custom_call_target="tpu_custom_call" | custom-call | tf_op jit(solution)/shard_map/pallas_call | solution.py:545

commit v6 on v5

--- a/solution.py
+++ b/solution.py
@@ -235,16 +235,22 @@
                 at = (side * 6 + part) * 16
                 ghost[at:at + 16, :] = out[side * 16:side * 16 + 16, part * 128:part * 128 + 128]
 
-    def fetch_near(turn):
+    def near_faces(turn):
         for peer in NEAR:
             copy_of(turn, peer, peer).wait()
         none = jnp.zeros((8, 384), jnp.float32)
         hi, mid, low = split3(jnp.concatenate([recvs[turn, c] if c in NEAR else none for c in range(8)], 0))
-        arrived = jnp.concatenate([hi, mid, low, jnp.zeros_like(low)], 0)
+        return jnp.concatenate([hi, mid, low, jnp.zeros_like(low)], 0)
+
+    def put_near(arrived, half):
         fold = jnp.where(lane_ids[:96] >= 64.0, lane_ids[:96] - 64.0, lane_ids[:96])
+        pick = as_one(far_col[...] + 4.0 * half == fold)
+        return dot(jnp.concatenate([pick, pick], 1), arrived)
+
+    def fetch_near(turn):
+        arrived = near_faces(turn)
         for half in range(2):
-            pick = as_one(far_col[...] + 4.0 * half == fold)
-            out = dot(jnp.concatenate([pick, pick], 1), arrived)
+            out = put_near(arrived, half)
             for side in range(6):
                 for part in range(3):
                     at = (side * 6 + half * 3 + part) * 16
@@ -396,7 +402,6 @@
     pick = as_one(jnp.logical_and(pick, (lane_bricks >> 4) == (out_z & 7)))
     turns = sorted(range(1, n_gz), key=lambda turn: abs(2 * turn - n_gz))
 
-    fetch_near(STEPS)
 
     def rim(axis, high, tile, edge):
         side = 2 * axis + high
@@ -431,34 +436,38 @@
             sigma[rows_of(0, z, tile), :] = grad_z
             sigma[rows_of(1, z, tile), :] = jnp.where(jnp.abs(here) < BAND_WIDTH, wave * wave * (2.0 / 3.0), 0.0)
 
+    rims = put_near(near_faces(STEPS)[:, :256], 0)
     copy_of(STEPS, FAR, FAR).wait()
-    far_rim = put_far(recvs[STEPS, FAR, :, :256])
-    turned = dot(jnp.concatenate(split3(far_rim[:32]), 1), swap)
+    rims = rims + put_far(recvs[STEPS, FAR, :, :256])
+    turned = dot(jnp.concatenate(split3(rims[:32]), 1), swap)
     groups = lax.broadcasted_iota(jnp.int32, (16, 128), 1)
     y_ids, x_ids = groups & 15, groups >> 4
 
-    def moved_to(mask, values, by):
-        return jnp.where(mask, pltpu.roll(values, by % 128, 1) if by % 128 else values, 0.0)
+    def moved(values, by):
+        return pltpu.roll(values, by % 128, 1) if by % 128 else values
 
     for tile in range(2):
         edge = 7 * tile
         held = None
+        low_y = rims[32:48, tile * 128:tile * 128 + 128]
+        high_y = moved(rims[48:64, tile * 128:tile * 128 + 128], 15)
         for z in range(16):
             at = z // 8 * 128
-            add_x = moved_to(x_ids == edge, turned[tile * 16:tile * 16 + 16, at:at + 128], 16 * (edge - z % 8))
+            add_x = moved(turned[tile * 16:tile * 16 + 16, at:at + 128], 16 * (edge - z % 8))
+            add_x = jnp.where(x_ids == edge, add_x, 0.0)
+            add_y = moved(jnp.where(y_ids == z, low_y, high_y), -z)
+            add_y = jnp.where(jnp.logical_or(y_ids == 0, y_ids == 15), add_y, 0.0)
             at = tile * 128
-            low_y = moved_to(y_ids == 0, far_rim[32:48, at:at + 128], -z)
-            high_y = moved_to(y_ids == 15, far_rim[48:64, at:at + 128], 15 - z)
-            lap = (grad[rows_of(0, z, tile), :] + add_x) + (low_y + high_y)
+            lap = grad[rows_of(0, z, tile), :] + (add_x + add_y)
             grad_x = grad[rows_of(1, z, tile), :] + (add_x if tile else -add_x)
-            grad_y = grad[rows_of(2, z, tile), :] + (high_y - low_y)
+            grad_y = grad[rows_of(2, z, tile), :] + jnp.where(y_ids == 0, -add_y, add_y)
             grad_z = sigma[rows_of(0, z, tile), :]
             if z == 0:
-                lap = lap + far_rim[64:80, at:at + 128]
-                grad_z = grad_z - far_rim[64:80, at:at + 128]
+                lap = lap + rims[64:80, at:at + 128]
+                grad_z = grad_z - rims[64:80, at:at + 128]
             if z == 15:
-                lap = lap + far_rim[80:96, at:at + 128]
-                grad_z = grad_z + far_rim[80:96, at:at + 128]
+                lap = lap + rims[80:96, at:at + 128]
+                grad_z = grad_z + rims[80:96, at:at + 128]
             lap = lap * sigma[rows_of(1, z, tile), :]
             forces = [lap * grad_x, lap * grad_y, lap * grad_z]
             if z % 2 == 0:

time: 64 us -> 62.5 us (0.977)
  Pallas kernels: 62.6 us -> 61.1 us
    pallas_call x1, Pallas kernels: 61.9 us -> 60.3 us  [shards(): pl.pallas_call(functools.partial(kernel, n_gx, n_gz), out_shape=(jax.Shap...]
where the time goes in v6:
time: 62.5 us; the launch traced here: 62.3 us
  Pallas kernels  61.1 us (98%)
  between operations  1.28 us (2%)
    pallas_call x1, Pallas kernels, shards(): pl.pallas_call(functools.partial(kernel, n_gx, n_gz), out_shape=(jax.Shap...  60.3 us

profile of v6, /device:TPU:1, one launch (start us, length us, event | category | flops | bytes accessed | tf_op | source)
XLA Modules:
  0.0 62.3 jit_solution(13406001067148484120)
XLA Ops:
  1.3 60.3 %shard_map.59 = (f32[16,4096]{1,0:T(8,128)S(1)}, f32[4,3,4,256]{3,2,1,0:T(4,128)S(1)}) custom-call(s32[6,16]{1,0:T(8,128)} %bitcast.1, s32[1]{0:T(128)S(6)} %copy.6.live, s32[16]{0:T(128)} %target_in.1, f32[16,4096]{1,0:T(8,128)} %level.1), custom_call_target="tpu_custom_call" | custom-call | tf_op jit(solution)/shard_map/pallas_call | solution.py:521
  61.6 0.7 %shard_map.60 = (f32[16,4096]{1,0:T(8,128)}, f32[4,3,4,256]{3,2,1,0:T(4,128)}) custom-call(f32[16,4096]{1,0:T(8,128)S(1)} %get-tuple-element.4.level, f32[4,3,4,256]{3,2,1,0:T(4,128)S(1)} %get-tuple-element.5.force), custom_call_target="tpu_custom_call" | custom-call | tf_op jit(solution)/shard_map/pallas_call | solution.py:554

commit v7 on v6

--- a/solution.py
+++ b/solution.py
@@ -26,14 +26,25 @@
     return 7 if peer == 7 else 6 - peer
 
 
+def roll_by(values, by):
+    return pltpu.roll(values, by % 128, 1) if by % 128 else values
+
+
+def pick_tree(rolled, masks):
+    count = len(rolled)
+    moved = [rolled[-i % count] for i in range(count)]
+    for bit, mask in enumerate(masks):
+        moved = [jnp.where(mask, moved[(i - (1 << bit)) % count], moved[i]) for i in range(count)]
+    return moved
+
+
 def exchange(values, width, masks):
-    count = len(values)
-    bits = count.bit_length() - 1
-    rolled = [v if j == 0 else pltpu.roll(v, j * width, 1) for j, v in enumerate(values)]
-    moved = [rolled[-i % count] for i in range(count)]
-    for bit in range(bits):
-        moved = [jnp.where(masks[bit], moved[(i - (1 << bit)) % count], moved[i]) for i in range(count)]
-    return [v if i == 0 else pltpu.roll(v, 128 - i * width, 1) for i, v in enumerate(moved)]
+    moved = pick_tree([roll_by(v, j * width) for j, v in enumerate(values)], masks)
+    return [roll_by(v, -i * width) for i, v in enumerate(moved)]
+
+
+def is_edge(position):
+    return min(position, 15 - position) < 3
 
 
 def lane_masks(rows, width, bits):
@@ -172,17 +183,25 @@
             faces[side * 16:side * 16 + 16, at:at + 128] = value
 
     def spread(tile, x_of):
-        ys = []
+        halves = []
         for ytile in range(2):
-            ys += exchange([x_of(i, ytile) for i in range(8)], 16, coarse_masks)
-        for y in range(16):
-            u[rows_of(1, y, tile), :] = ys[y]
-            keep_face(1, y, tile, ys[y])
-        zs = exchange(ys, 1, fine_masks)
-        for z in range(16):
-            u[rows_of(2, z, tile), :] = zs[z]
-            keep_face(2, z, tile, zs[z])
-        return ys, zs
+            halves += pick_tree([roll_by(x_of(i, ytile), 16 * i) for i in range(8)], coarse_masks)
+        zs = pick_tree([roll_by(halves[y], y - 16 * (y % 8)) for y in range(16)], fine_masks)
+        for axis, values, width in ((1, halves, 16), (2, zs, 1)):
+            for p in range(16):
+                value = values[p]
+                if is_edge(p):
+                    value = roll_by(value, -(p * width))
+                    keep_face(axis, p, tile, value)
+                u[rows_of(axis, p, tile), :] = value
+
+    def settle():
+        for tile in range(2):
+            for p in range(3, 13):
+                for axis, width in ((1, 16), (2, 1)):
+                    value = roll_by(u[rows_of(axis, p, tile), :], -(p * width))
+                    u[rows_of(axis, p, tile), :] = value
+                    keep_face(axis, p, tile, value)
 
     load_target.wait()
     load.wait()
@@ -197,10 +216,11 @@
                 sigma[rows_of(0, x, ytile), :] = jnp.where(value > 0.0, 1.0, -1.0)
                 speed[rows_of(0, x, ytile), :] = 0.1 * value * lax.rsqrt(value * value + 1.0)
                 tops[i, ytile] = value
-        ys, zs = spread(tile, lambda i, ytile: tops[i, ytile])
-        for p in range(16):
-            sigma[rows_of(1, p, tile), :] = jnp.where(ys[p] > 0.0, 1.0, -1.0)
-            sigma[rows_of(2, p, tile), :] = jnp.where(zs[p] > 0.0, 1.0, -1.0)
+        spread(tile, lambda i, ytile: tops[i, ytile])
+    settle()
+    for axis in (1, 2):
+        rows = pl.ds(axis * AXIS_ROWS, AXIS_ROWS)
+        sigma[rows, :] = jnp.where(u[rows, :] > 0.0, 1.0, -1.0)
 
     for peer in PEERS:
         pltpu.make_async_remote_copy(
@@ -324,11 +344,11 @@
             values[16 + i] = ghosts_at(axis, 1, i, column, values[15])
         weno_axis(values, 13, 16, signs, store)
 
+    serve(0)
     first = own_cells()[:, :768]
     far_sigma[...] = jnp.where(first > 0.0, 1.0, -1.0)
 
     def step(turn, carry):
-        serve(turn)
 
         def inner(index, c):
             weno_part(index, 3, 13)
@@ -339,6 +359,12 @@
             return c
 
         lax.fori_loop(0, 12, inner, 0)
+        for tile in range(2):
+            for p in range(3, 13):
+                for axis, width in ((1, 16), (2, 1)):
+                    if p * width % 128:
+                        rows = rows_of(axis, p, tile)
+                        grad[rows, :] = roll_by(grad[rows, :], p * width)
         own = own_cells()
         fetch_near(turn)
         lax.fori_loop(0, 12, outer, 0)
@@ -354,24 +380,30 @@
             return jnp.where(is_far(side), fixed[side * 16:side * 16 + 16, at:at + 128], value)
 
         for tile in range(2):
-            sums = exchange([grad_at(2, z, tile) for z in range(16)], 1, fine_masks)
-            sums = [sums[y] + grad_at(1, y, tile) for y in range(16)]
+            zs = [grad_at(2, z, tile) for z in range(16)]
+            zs = pick_tree([roll_by(v, z) if is_edge(z) else v for z, v in enumerate(zs)], fine_masks)
+            sums = []
+            for y in range(16):
+                value = grad_at(1, y, tile)
+                value = roll_by(value, 16 * y) if is_edge(y) else value
+                sums.append(roll_by(zs[y], 16 * y - y) + value)
             fresh = {}
             for ytile in range(2):
-                xs = exchange(sums[ytile * 8:ytile * 8 + 8], 16, coarse_masks)
+                xs = pick_tree(sums[ytile * 8:ytile * 8 + 8], coarse_masks)
                 for i in range(8):
                     rows = rows_of(0, tile * 8 + i, ytile)
-                    steep = jnp.sqrt(xs[i] + grad_at(0, tile * 8 + i, ytile))
+                    steep = jnp.sqrt(roll_by(xs[i], -16 * i) + grad_at(0, tile * 8 + i, ytile))
                     value = u[rows, :] - speed[rows, :] * (steep - 3.0)
                     u[rows, :] = value
                     keep_face(0, tile * 8 + i, ytile, value)
                     fresh[i, ytile] = value
             spread(tile, lambda i, ytile: fresh[i, ytile])
+        serve(turn + 1)
+        settle()
         return carry
 
     lax.fori_loop(0, STEPS, step, 0)
 
-    serve(STEPS)
     keep = lax.broadcasted_iota(jnp.int32, (16, 128), 0) < live[0]
     for x in range(16):
         for ytile in range(2):
@@ -443,19 +475,16 @@
     groups = lax.broadcasted_iota(jnp.int32, (16, 128), 1)
     y_ids, x_ids = groups & 15, groups >> 4
 
-    def moved(values, by):
-        return pltpu.roll(values, by % 128, 1) if by % 128 else values
-
     for tile in range(2):
         edge = 7 * tile
         held = None
         low_y = rims[32:48, tile * 128:tile * 128 + 128]
-        high_y = moved(rims[48:64, tile * 128:tile * 128 + 128], 15)
+        high_y = roll_by(rims[48:64, tile * 128:tile * 128 + 128], 15)
         for z in range(16):
             at = z // 8 * 128
-            add_x = moved(turned[tile * 16:tile * 16 + 16, at:at + 128], 16 * (edge - z % 8))
+            add_x = roll_by(turned[tile * 16:tile * 16 + 16, at:at + 128], 16 * (edge - z % 8))
             add_x = jnp.where(x_ids == edge, add_x, 0.0)
-            add_y = moved(jnp.where(y_ids == z, low_y, high_y), -z)
+            add_y = roll_by(jnp.where(y_ids == z, low_y, high_y), -z)
             add_y = jnp.where(jnp.logical_or(y_ids == 0, y_ids == 15), add_y, 0.0)
             at = tile * 128
             lap = grad[rows_of(0, z, tile), :] + (add_x + add_y)

time: 62.5 us -> 61.5 us (0.984)
  Pallas kernels: 61.1 us -> 60.1 us
    pallas_call x1, Pallas kernels: 60.3 us -> 59.4 us  [shards(): pl.pallas_call(functools.partial(kernel, n_gx, n_gz), out_shape=(jax.Shap...]
where the time goes in v7:
time: 61.5 us; the launch traced here: 61.4 us
  Pallas kernels  60.1 us (98%)
  between operations  1.28 us (2%)
    pallas_call x1, Pallas kernels, shards(): pl.pallas_call(functools.partial(kernel, n_gx, n_gz), out_shape=(jax.Shap...  59.4 us

profile of v7, /device:TPU:1, one launch (start us, length us, event | category | flops | bytes accessed | tf_op | source)
XLA Modules:
  0.0 61.4 jit_solution(490263567018104378)
XLA Ops:
  1.3 59.4 %shard_map.59 = (f32[16,4096]{1,0:T(8,128)S(1)}, f32[4,3,4,256]{3,2,1,0:T(4,128)S(1)}) custom-call(s32[6,16]{1,0:T(8,128)} %bitcast.1, s32[1]{0:T(128)S(6)} %copy.6.live, s32[16]{0:T(128)} %target_in.1, f32[16,4096]{1,0:T(8,128)} %level.1), custom_call_target="tpu_custom_call" | custom-call | tf_op jit(solution)/shard_map/pallas_call | solution.py:550
  60.6 0.7 %shard_map.60 = (f32[16,4096]{1,0:T(8,128)}, f32[4,3,4,256]{3,2,1,0:T(4,128)}) custom-call(f32[16,4096]{1,0:T(8,128)S(1)} %get-tuple-element.4.level, f32[4,3,4,256]{3,2,1,0:T(4,128)S(1)} %get-tuple-element.5.force), custom_call_target="tpu_custom_call" | custom-call | tf_op jit(solution)/shard_map/pallas_call | solution.py:583

commit v8 on v7

--- a/solution.py
+++ b/solution.py
@@ -109,7 +109,7 @@
 
 
 def kernel(n_gx, n_gz, table, live, target_in, level, level_out, part_out,
-           nb, target, start, u, faces, ghost, sigma, grad, speed, missing, near_col, far_col, take, far_sigma, force, request, heard,
+           nb, target, start, u, faces, ghost, sigma, grad, speed, lean, missing, near_col, far_col, take, far_sigma, force, request, heard,
            sends, recvs, fsend, frecv,
            table_loaded, target_loaded, loaded, request_sent, request_got, sent, got, fsent, fgot):
     me = lax.axis_index("gx")
@@ -185,7 +185,7 @@
     def spread(tile, x_of):
         halves = []
         for ytile in range(2):
-            halves += pick_tree([roll_by(x_of(i, ytile), 16 * i) for i in range(8)], coarse_masks)
+            halves += pick_tree([x_of(i, ytile) for i in range(8)], coarse_masks)
         zs = pick_tree([roll_by(halves[y], y - 16 * (y % 8)) for y in range(16)], fine_masks)
         for axis, values, width in ((1, halves, 16), (2, zs, 1)):
             for p in range(16):
@@ -195,10 +195,20 @@
                     keep_face(axis, p, tile, value)
                 u[rows_of(axis, p, tile), :] = value
 
+    def put_x(x, ytile, rolled):
+        rows = rows_of(0, x, ytile)
+        lean[rows, :] = rolled
+        if is_edge(x):
+            value = roll_by(rolled, -16 * x)
+            keep_face(0, x, ytile, value)
+            u[rows, :] = value
+        else:
+            u[rows, :] = rolled
+
     def settle():
         for tile in range(2):
             for p in range(3, 13):
-                for axis, width in ((1, 16), (2, 1)):
+                for axis, width in ((0, 16), (1, 16), (2, 1)):
                     value = roll_by(u[rows_of(axis, p, tile), :], -(p * width))
                     u[rows_of(axis, p, tile), :] = value
                     keep_face(axis, p, tile, value)
@@ -211,11 +221,11 @@
             for ytile in range(2):
                 x = tile * 8 + i
                 value = start[:, x * 256 + ytile * 128:x * 256 + ytile * 128 + 128]
-                u[rows_of(0, x, ytile), :] = value
-                keep_face(0, x, ytile, value)
                 sigma[rows_of(0, x, ytile), :] = jnp.where(value > 0.0, 1.0, -1.0)
-                speed[rows_of(0, x, ytile), :] = 0.1 * value * lax.rsqrt(value * value + 1.0)
-                tops[i, ytile] = value
+                rolled = roll_by(value, 16 * x)
+                speed[rows_of(0, x, ytile), :] = 0.1 * rolled * lax.rsqrt(rolled * rolled + 1.0)
+                put_x(x, ytile, rolled)
+                tops[i, ytile] = rolled
         spread(tile, lambda i, ytile: tops[i, ytile])
     settle()
     for axis in (1, 2):
@@ -361,7 +371,7 @@
         lax.fori_loop(0, 12, inner, 0)
         for tile in range(2):
             for p in range(3, 13):
-                for axis, width in ((1, 16), (2, 1)):
+                for axis, width in ((0, 16), (1, 16), (2, 1)):
                     if p * width % 128:
                         rows = rows_of(axis, p, tile)
                         grad[rows, :] = roll_by(grad[rows, :], p * width)
@@ -392,10 +402,10 @@
                 xs = pick_tree(sums[ytile * 8:ytile * 8 + 8], coarse_masks)
                 for i in range(8):
                     rows = rows_of(0, tile * 8 + i, ytile)
-                    steep = jnp.sqrt(roll_by(xs[i], -16 * i) + grad_at(0, tile * 8 + i, ytile))
-                    value = u[rows, :] - speed[rows, :] * (steep - 3.0)
-                    u[rows, :] = value
-                    keep_face(0, tile * 8 + i, ytile, value)
+                    here = grad_at(0, tile * 8 + i, ytile)
+                    here = roll_by(here, 16 * i) if is_edge(tile * 8 + i) else here
+                    value = lean[rows, :] - speed[rows, :] * (jnp.sqrt(xs[i] + here) - 3.0)
+                    put_x(tile * 8 + i, ytile, value)
                     fresh[i, ytile] = value
             spread(tile, lambda i, ytile: fresh[i, ytile])
         serve(turn + 1)
@@ -562,6 +572,7 @@
             pltpu.VMEM((3 * AXIS_ROWS, 128), f32),
             pltpu.VMEM((3 * AXIS_ROWS, 128), f32),
             pltpu.VMEM((AXIS_ROWS, 128), f32),
+            pltpu.VMEM((AXIS_ROWS, 128), f32),
             pltpu.VMEM((96, 128), f32),
             pltpu.VMEM((96, 128), f32),
             pltpu.VMEM((96, 128), f32),

time: 61.5 us -> 61.4 us (level)
  no operation moved by 1% of the time
where the time goes in v8:
time: 61.4 us; the launch traced here: 61.2 us
  Pallas kernels  59.9 us (98%)
  between operations  1.28 us (2%)
    pallas_call x1, Pallas kernels, shards(): pl.pallas_call(functools.partial(kernel, n_gx, n_gz), out_shape=(jax.Shap...  59.2 us

profile of v8, /device:TPU:1, one launch (start us, length us, event | category | flops | bytes accessed | tf_op | source)
XLA Modules:
  0.0 61.2 jit_solution(1719398310646563579)
XLA Ops:
  1.3 59.2 %shard_map.59 = (f32[16,4096]{1,0:T(8,128)S(1)}, f32[4,3,4,256]{3,2,1,0:T(4,128)S(1)}) custom-call(s32[6,16]{1,0:T(8,128)} %bitcast.1, s32[1]{0:T(128)S(6)} %copy.6.live, s32[16]{0:T(128)} %target_in.1, f32[16,4096]{1,0:T(8,128)} %level.1), custom_call_target="tpu_custom_call" | custom-call | tf_op jit(solution)/shard_map/pallas_call | solution.py:560
  60.5 0.7 %shard_map.60 = (f32[16,4096]{1,0:T(8,128)}, f32[4,3,4,256]{3,2,1,0:T(4,128)}) custom-call(f32[16,4096]{1,0:T(8,128)S(1)} %get-tuple-element.4.level, f32[4,3,4,256]{3,2,1,0:T(4,128)S(1)} %get-tuple-element.5.force), custom_call_target="tpu_custom_call" | custom-call | tf_op jit(solution)/shard_map/pallas_call | solution.py:594
